TPU v7x, 32 devices: a whole 2x2x4 slice. The times are simulated.
32 devices in a mesh: rep: 2 (over y), tp: 4 (over x, core), cp: 4 (over z).
Axes of the slice: x: 2, y: 2, z: 4, core: 2. Of those that a mesh axis runs over, the one named last changes fastest.
Arguments:
- tokens: bfloat16 [2, 3072, 1280], P('rep', 'cp', 'tp'), may hold values from -6 to 6
- qkv_weight: float32 [1280, 3, 1280], P(('rep', 'cp'), None, 'tp'), may hold values from -0.3 to 0.3
- out_weight: float32 [1280, 1280], P('tp', ('rep', 'cp')), may hold values from -0.3 to 0.3
- gate_up_weight: float32 [1280, 2, 5120], P(('rep', 'cp'), None, 'tp'), may hold values from -0.3 to 0.3
- down_weight: float32 [5120, 1280], P('tp', ('rep', 'cp')), may hold values from -0.15 to 0.15
- qk_scale: float32 [1280], P('tp'), may hold values from 0.9 to 6.6, as said below
- attn_rate: float32 [1280], replicated, may hold values from 0.05 to 0.6
- mlp_rate: float32 [1280], replicated, may hold values from 0.05 to 0.6
- up_scale: float32 [5120], P('tp'), may hold values from 0.5 to 2
- gate_scale: float32 [5120], P('tp'), may hold values from 0.5 to 2
- segment_ids: int32 [2, 3072], P('rep'), may hold values from 0 to 23, never falling along the last dimension, each value on 1 to 512 neighbouring positions
Outputs:
- next_state: bfloat16 [2, 3072, 1280], P('rep', 'cp', 'tp')
Inputs may be any that keep to these rules, and one draw needn't show every extreme that they name: `segment_ids`: along each replica's row the ids never fall, and each prompt covers 1 to 512 positions; some prompt covers exactly 512. `qk_scale`: positive channel scales.
All inputs are finite; a program needn't handle non-finite values.
Results may differ from a plain program's by a relative error of at most 0.015.
Values may be sent and summed in bfloat16 or wider, within the bound.
A program may use at most 128 MiB of HBM per device.

v0:
```python
import math

import jax
import jax.numpy as jnp
from jax import lax
from jax.sharding import PartitionSpec as P

D = 1280
HD = 64


EPS = 1e-06


def shifted(block, axis, distance):
    devices = range(lax.axis_size(axis))
    route = [(i - distance, i) for i in devices if i - distance in devices]
    return lax.ppermute(block, axis, route)


def unit_rows(array):
    return array * lax.rsqrt(jnp.sum(array * array, axis=-1, keepdims=True) + EPS)


def share_unit(array):
    totals = lax.psum(jnp.sum(array * array, axis=-1), "tp")
    return array * lax.rsqrt(totals + EPS)[:, None]


def rotate(array, position):
    half_dim = array.shape[-1] // 2
    frequency = jnp.exp(
        -math.log(10000.0) * jnp.arange(half_dim, dtype=jnp.float32) * 2.0 / array.shape[-1]
    )
    angles = position.astype(jnp.float32)[:, None] * frequency[None, :]
    cosine = jnp.cos(angles)[:, None, :]
    sine_part = jnp.sin(angles)[:, None, :]
    first_half = array[..., :half_dim]
    second_half = array[..., half_dim:]
    return jnp.concatenate(
        [
            first_half * cosine - second_half * sine_part,
            first_half * sine_part + second_half * cosine,
        ],
        axis=-1,
    )


def stream_positions(segment):
    order_index = jnp.arange(segment.shape[0], dtype=jnp.int32)
    earlier = jnp.concatenate([segment[:1], segment[:-1]])
    boundary = jnp.where(segment != earlier, order_index, jnp.zeros_like(order_index))
    return order_index - lax.cummax(boundary)


def fold_rows(left, piece):
    return jnp.dot(left, piece.reshape(piece.shape[0], -1), preferred_element_type=jnp.float32)


def right_product(left, piece):
    return jnp.dot(left, piece, preferred_element_type=jnp.float32)


def body(
    tokens,
    qkv_weight,
    out_weight,
    gate_up_weight,
    down_weight,
    qk_scale,
    attn_rate,
    mlp_rate,
    up_scale,
    gate_scale,
    segment_ids,
):
    rows = tokens.shape[1]
    local = tokens.shape[2]
    heads = local // HD
    hidden_local = gate_up_weight.shape[2]
    tp_index = lax.axis_index("tp")
    cp_index = lax.axis_index("cp")
    whole_tokens = lax.all_gather(tokens, "tp", axis=2, tiled=True)[0]
    state = unit_rows(whole_tokens.astype(jnp.float32))
    state_in = state.astype(jnp.bfloat16)
    sums = lax.psum(
        (
            jnp.sum(qkv_weight * qkv_weight, axis=0),
            jnp.sum(out_weight * out_weight, axis=1),
            jnp.sum(gate_up_weight * gate_up_weight, axis=0),
            jnp.sum(down_weight * down_weight, axis=1),
        ),
        ("rep", "cp"),
    )
    qkv_norm = (qkv_weight * lax.rsqrt(sums[0] + EPS)[None]).astype(jnp.bfloat16)
    out_norm = (out_weight * lax.rsqrt(sums[1] + EPS)[:, None]).astype(jnp.bfloat16)
    gate_up_norm = (gate_up_weight * lax.rsqrt(sums[2] + EPS)[None]).astype(jnp.bfloat16)
    down_norm = (down_weight * lax.rsqrt(sums[3] + EPS)[:, None]).astype(jnp.bfloat16)
    projected = fold_rows(state_in, lax.all_gather(qkv_norm, ("rep", "cp"), axis=0, tiled=True))
    projected = projected.reshape(rows, 3, heads, HD)
    scale_table = qk_scale.reshape(heads, HD)
    query = (scale_table * unit_rows(projected[:, 0])).astype(jnp.bfloat16)
    keys = (scale_table * unit_rows(projected[:, 1])).astype(jnp.bfloat16)
    values = projected[:, 2].astype(jnp.bfloat16)
    prev_keys, prev_values = shifted((keys, values), "cp", 1)
    segment = segment_ids[0]
    position = stream_positions(segment)
    own_start = cp_index * rows
    prev_start = jnp.maximum(own_start - rows, 0)
    own_pos = lax.dynamic_slice_in_dim(position, own_start, rows)
    prev_pos = lax.dynamic_slice_in_dim(position, prev_start, rows)
    own_seg = lax.dynamic_slice_in_dim(segment, own_start, rows)
    prev_seg = lax.dynamic_slice_in_dim(segment, prev_start, rows)
    query_rot = rotate(query.astype(jnp.float32), own_pos).astype(jnp.bfloat16)
    keys_rot = jnp.concatenate(
        [
            rotate(prev_keys.astype(jnp.float32), prev_pos),
            rotate(keys.astype(jnp.float32), own_pos),
        ],
        axis=0,
    ).astype(jnp.bfloat16)
    key_values = jnp.concatenate([prev_values, values], axis=0)
    key_seg = jnp.concatenate([prev_seg, own_seg])
    key_order = jnp.arange(2 * rows, dtype=jnp.int32)
    query_order = jnp.arange(rows, dtype=jnp.int32) + rows
    allowed = (
        (own_seg[:, None] == key_seg[None, :])
        & (query_order[:, None] >= key_order[None, :])
        & ((key_order[None, :] >= rows) | (cp_index > 0))
    )
    scores = jnp.einsum(
        "qhd,khd->hqk", query_rot, keys_rot, preferred_element_type=jnp.float32
    ) * math.sqrt(HD)
    scores = jnp.where(allowed[None], scores, -1e30)
    exponent = jnp.exp(scores - jnp.max(scores, axis=-1, keepdims=True))
    probs = (exponent / jnp.sum(exponent, axis=-1, keepdims=True)).astype(jnp.bfloat16)
    attended = (
        jnp.einsum("hqk,khd->qhd", probs, key_values, preferred_element_type=jnp.float32)
        .astype(jnp.bfloat16)
        .reshape(rows, local)
    )
    attn_part = right_product(attended, lax.all_gather(out_norm, ("rep", "cp"), axis=1, tiled=True))
    attn_block = lax.psum_scatter(attn_part, "tp", scatter_dimension=1, tiled=True)
    state_block = lax.dynamic_slice_in_dim(state, tp_index * local, local, 1)
    rate_block = lax.dynamic_slice_in_dim(attn_rate, tp_index * local, local, 0)
    mixed = share_unit(state_block + rate_block * (share_unit(attn_block) - state_block))
    mixed_in = lax.all_gather(mixed.astype(jnp.bfloat16), "tp", axis=1, tiled=True)
    gate_up = fold_rows(mixed_in, lax.all_gather(gate_up_norm, ("rep", "cp"), axis=0, tiled=True))
    up_branch = gate_up[:, :hidden_local] * up_scale
    gate_branch = gate_up[:, hidden_local:] * gate_scale * math.sqrt(D)
    inner = (up_branch * jax.nn.silu(gate_branch)).astype(jnp.bfloat16)
    mlp_part = right_product(inner, lax.all_gather(down_norm, ("rep", "cp"), axis=1, tiled=True))
    mlp_block = lax.psum_scatter(mlp_part, "tp", scatter_dimension=1, tiled=True)
    mlp_rate_block = lax.dynamic_slice_in_dim(mlp_rate, tp_index * local, local, 0)
    result = math.sqrt(D) * share_unit(mixed + mlp_rate_block * (share_unit(mlp_block) - mixed))
    return result.astype(jnp.bfloat16)[None]


def solution(mesh):
    in_specs = (
        P("rep", "cp", "tp"),
        P(("rep", "cp"), None, "tp"),
        P("tp", ("rep", "cp")),
        P(("rep", "cp"), None, "tp"),
        P("tp", ("rep", "cp")),
        P("tp"),
        P(),
        P(),
        P("tp"),
        P("tp"),
        P("rep", None),
    )
    out_specs = P("rep", "cp", "tp")
    return jax.shard_map(body, mesh=mesh, in_specs=in_specs, out_specs=out_specs, check_vma=False)
```

profile of v0, /device:TPU:1, one launch (start us, length us, event | category | flops | bytes accessed | tf_op | source)
XLA Modules:
  0.0 478.5 jit_solution(3946804541425593)
XLA Ops:
  12.9 31.9 %all-reduce = (f32[1280]{0:T(1024)}, f32[320]{0:T(512)S(1)}, f32[3,320]{1,0:T(4,128)S(1)}, f32[2,1280]{1,0:T(2,128)S(1)}) all-reduce(f32[1280]{0:T(1024)S(1)} %multiply_reduce_fusion.8, f32[320]{0:T(512)S(1)} %multiply_reduce_fusion.10, f32[3,320]{1,0:T(4,128)S(1)} %multiply_reduce_fusion.9, ...), channel_id=1, replica_groups=mesh['rep'=2,'tp'=4,'cp'=4] {'rep','cp'}, use_global_device_ids=true, to_apply=%region_19.20 | all-reduce | flops 5120 | bytes 40960 | tf_op jit(solution)/shard_map/psum | solution.py:86
  49.2 34.9 %all_gather.20 = bf16[320,1280]{0,1:T(8,128)(2,1)S(1)} all-gather(bf16[320,160]{0,1:T(8,128)(2,1)S(1)} %multiply_convert_fusion.7), channel_id=1, replica_groups=mesh['rep'=2,'tp'=4,'cp'=4] {'rep','cp'}, dimensions={1}, use_global_device_ids=true | all-gather | bytes 921600 | tf_op jit(solution)/shard_map/all_gather | solution.py:142
  84.1 3.2 fusion.7
  89.4 27.5 %all-gather.8.cloned.1.call-done = bf16[1280,3,320]{2,0,1:T(8,128)(2,1)} async-done(((bf16[160,3,320]{2,0,1:T(8,128)(2,1)}), bf16[1280,3,320]{2,0,1:T(8,128)(2,1)}) %all-gather.8.cloned.1.call-update) | async-done | bytes 2457616 | tf_op jit(solution)/shard_map/all_gather | solution.py:99
  116.9 5.3 %copy.15 = bf16[1280,3,320]{0,2,1:T(8,128)(2,1)} copy(bf16[1280,3,320]{2,0,1:T(8,128)(2,1)} %all-gather.8.cloned.1.call-done) | data formatting | bytes 4915200 | tf_op jit(solution)/shard_map/all_gather | solution.py:99
  122.2 3.9 fusion.15
  126.7 4.5 collective-permute-start.1
  131.2 4.1 collective-permute-start
  136.5 3.8 collective-permute-done.1
  141.3 9.5 %fusion.46 = f32[5,768]{1,0:T(8,128)S(1)} fusion(pred[768,1536]{1,0:T(8,128)(4,1)} %fusion.7, bf16[768,5,32]{0,2,1:T(8,128)(2,1)} %get-tuple-element.24, bf16[768,5,32]{0,2,1:T(8,128)(2,1)} %get-tuple-element.25, bf16[768,5,32]{0,2,1:T(8,128)(2,1)} %get-tuple-element.21, bf16[768,5,32]{0,2,1:T(8,128)(2,1)} %get-tuple-element.20, ...), kind=kOutput, calls=%fused_computation.106 | convolution fusion | flops 783484416 | bytes 2669568 | tf_op jit(solution)/shard_map/sub | solution.py:135
  150.8 12.4 %fusion.20 = bf16[5,64,768]{2,1,0:T(8,128)(2,1)} fusion(f32[5,768]{1,0:T(8,128)S(1)} %fusion.46, bf16[768,5,64]{0,2,1:T(8,128)(2,1)S(1)} %fusion.26, bf16[768,5,64]{0,2,1:T(8,128)(2,1)} %collective-permute-done, pred[768,1536]{1,0:T(8,128)(4,1)} %fusion.7, bf16[768,5,32]{0,2,1:T(8,128)(2,1)} %get-tuple-element.24, ...), kind=kOutput, calls=%fused_computation.28 | convolution fusion | flops 1546573056 | bytes 4144128 | tf_op jit(solution)/shard_map/hqk,khd->qhd/dot_general | solution.py:138
  163.2 4.2 fusion.48
  173.5 40.2 %reduce-scatter.3.cloned.1.call-done = f32[768,320]{0,1:T(8,128)} async-done(((f32[768,1280]{0,1:T(8,128)}), f32[768,320]{0,1:T(8,128)}) %reduce-scatter.3.cloned.1.call-update) | async-done | bytes 983056 | tf_op jit(solution)/shard_map/reduce_scatter | solution.py:143
  215.0 5.7 %psum.58 = f32[768]{0:T(1024)S(1)} all-reduce(f32[768]{0:T(1024)S(1)} %multiply_reduce_fusion.5), channel_id=1, replica_groups=mesh['rep'=2,'tp'=4,'cp'=4] {'tp'}, use_global_device_ids=true, to_apply=%region_13.14 | all-reduce | flops 768 | bytes 6144 | tf_op jit(solution)/shard_map/psum | solution.py:26
  222.5 5.8 %psum.59 = f32[768]{0:T(1024)S(1)} all-reduce(f32[768]{0:T(1024)S(1)} %get-tuple-element.13), channel_id=1, replica_groups=mesh['rep'=2,'tp'=4,'cp'=4] {'tp'}, use_global_device_ids=true, to_apply=%region_15.16 | all-reduce | flops 768 | bytes 6144 | tf_op jit(solution)/shard_map/psum | solution.py:26
  230.4 87.4 %all-gather.12.cloned.1.call-done = bf16[1280,2,1280]{2,1,0:T(2,128)(2,1)} async-done(((bf16[160,2,1280]{2,1,0:T(2,128)(2,1)}), bf16[1280,2,1280]{2,1,0:T(2,128)(2,1)}) %all-gather.12.cloned.1.call-update) | async-done | bytes 6553616 | tf_op jit(solution)/shard_map/all_gather | solution.py:148
  317.7 6.9 %copy.19 = bf16[160,8,2,1280]{3,1,2,0:T(8,128)(2,1)} copy(bf16[160,8,2,1280]{3,2,1,0:T(2,128)(2,1)} %bitcast.56) | data formatting | bytes 13107200
  324.6 15.4 %all-gather.10.cloned.1.call-done = bf16[768,1280]{0,1:T(8,128)(2,1)} async-done(((bf16[768,320]{0,1:T(8,128)(2,1)}), bf16[768,1280]{0,1:T(8,128)(2,1)}) %all-gather.10.cloned.1.call-update) | async-done | bytes 1966096 | tf_op jit(solution)/shard_map/all_gather | solution.py:147
  340.1 10.6 %fusion.47 = f32[768,2560]{1,0:T(8,128)} fusion(bf16[768,1280]{0,1:T(8,128)(2,1)} %all-gather.10.cloned.1.call-done, bf16[1280,2560]{1,0:T(8,128)(2,1)} %bitcast.57), kind=kOutput, calls=%fused_computation.107 | convolution fusion | flops 5033164800 | bytes 16384000 | tf_op jit(solution)/shard_map/dot_general | solution.py:57
  350.7 52.3 %all-gather.14.cloned.1.call-done = bf16[1280,1280]{0,1:T(8,128)(2,1)} async-done(((bf16[1280,160]{0,1:T(8,128)(2,1)}), bf16[1280,1280]{0,1:T(8,128)(2,1)}) %all-gather.14.cloned.1.call-update) | async-done | bytes 3276816 | tf_op jit(solution)/shard_map/all_gather | solution.py:152
  403.0 9.1 %fusion.18 = f32[768,1280]{0,1:T(8,128)} fusion(bf16[1280,1280]{0,1:T(8,128)(2,1)} %all-gather.14.cloned.1.call-done, f32[768,2560]{1,0:T(8,128)} %fusion.47, f32[1280]{0:T(1024)S(1)} %copy-done.10, f32[1280]{0:T(1024)S(1)} %copy-done.11), kind=kOutput, calls=%fused_computation.25 | convolution fusion | flops 2525429760 | bytes 15083520 | tf_op jit(solution)/shard_map/dot_general | solution.py:61
  412.9 41.7 %reduce-scatter.5.cloned.1.call-done = f32[768,320]{0,1:T(8,128)} async-done(((f32[768,1280]{0,1:T(8,128)}), f32[768,320]{0,1:T(8,128)}) %reduce-scatter.5.cloned.1.call-update) | async-done | bytes 983056 | tf_op jit(solution)/shard_map/reduce_scatter | solution.py:153
  455.9 5.7 %psum.62 = f32[768]{0:T(1024)S(1)} all-reduce(f32[768]{0:T(1024)S(1)} %multiply_reduce_fusion.3), channel_id=1, replica_groups=mesh['rep'=2,'tp'=4,'cp'=4] {'tp'}, use_global_device_ids=true, to_apply=%region_22.23 | all-reduce | flops 768 | bytes 6144 | tf_op jit(solution)/shard_map/psum | solution.py:26
  463.2 5.8 %psum.63 = f32[768]{0:T(1024)S(1)} all-reduce(f32[768]{0:T(1024)S(1)} %multiply_reduce_fusion.2), channel_id=1, replica_groups=mesh['rep'=2,'tp'=4,'cp'=4] {'tp'}, use_global_device_ids=true, to_apply=%region_24.25 | all-reduce | flops 768 | bytes 6144 | tf_op jit(solution)/shard_map/psum | solution.py:26
  (89 shorter events, 32.7 us)
Async XLA Ops:
  6.5 41.2 %copy-start.3 = (f32[320,160]{0,1:T(8,128)S(1)}, f32[320,160]{0,1:T(8,128)}, u32[]{:S(2)}) copy-start(f32[320,160]{0,1:T(8,128)} %param.13) | copy-start | bytes 614404
  6.5 38.2 %copy-start.2 = (f32[160,3,320]{2,0,1:T(8,128)S(1)}, f32[160,3,320]{2,0,1:T(8,128)}, u32[]{:S(2)}) copy-start(f32[160,3,320]{2,0,1:T(8,128)} %param.12) | copy-start | bytes 1843204
  6.5 39.1 %copy-start.9 = (f32[320]{0:T(512)S(1)}, f32[320]{0:T(512)}, u32[]{:S(2)}) copy-start(f32[320]{0:T(512)} %param.16) | copy-start | bytes 3844
  6.5 39.2 %copy-start.7 = (s32[1,3072]{1,0:T(1,128)S(1)}, s32[1,3072]{1,0:T(1,128)}, u32[]{:S(2)}) copy-start(s32[1,3072]{1,0:T(1,128)} %param.21) | copy-start | bytes 36868
  6.5 80.7 %all-gather.6.cloned.1.call-start = ((), (), s32[]{:S(2)}) async-start(), calls=%async_computation.2 | async-start | bytes 2457600 | tf_op jit(solution)/shard_map/all_gather | solution.py:83
  7.3 109.7 %all-gather.8.cloned.1.call-start = ((), (), s32[]{:S(2)}) async-start(), calls=%async_computation.3 | async-start | bytes 3317760 | tf_op jit(solution)/shard_map/all_gather | solution.py:99
  45.6 168.1 %reduce-scatter.3.cloned.1.call-start = ((), (), s32[]{:S(2)}) async-start(), calls=%async_computation.4 | async-start | bytes 4915200 | tf_op jit(solution)/shard_map/reduce_scatter | solution.py:143
  87.3 34.9 %copy-start = (bf16[1,768,1280]{1,2,0:T(8,128)(2,1)S(1)}, bf16[1,768,1280]{1,2,0:T(8,128)(2,1)}, u32[]{:S(2)}) copy-start(bf16[1,768,1280]{1,2,0:T(8,128)(2,1)} %all-gather.6.cloned.1.call-done) | copy-start | bytes 5898244
  126.1 9.2 %copy-start.4 = (f32[768,32]{0,1:T(8,128)S(1)}, f32[768,32]{0,1:T(8,128)}, u32[]{:S(2)}) copy-start(f32[768,32]{0,1:T(8,128)} %get-tuple-element.33) | copy-start | bytes 294916
  126.4 14.0 %copy-start.5 = (f32[768,32]{0,1:T(8,128)S(1)}, f32[768,32]{0,1:T(8,128)}, u32[]{:S(2)}) copy-start(f32[768,32]{0,1:T(8,128)} %get-tuple-element.28) | copy-start | bytes 294916
  126.4 14.0 %copy-start.6 = (f32[768,32]{0,1:T(8,128)S(1)}, f32[768,32]{0,1:T(8,128)}, u32[]{:S(2)}) copy-start(f32[768,32]{0,1:T(8,128)} %get-tuple-element.29) | copy-start | bytes 294916
  126.7 13.6 %collective-permute-start.1 = (bf16[768,5,64]{0,2,1:T(8,128)(2,1)S(1)}, bf16[768,5,64]{0,2,1:T(8,128)(2,1)S(1)}, u32[]{:S(2)}, u32[]{:S(2)}) collective-permute-start(bf16[768,5,64]{0,2,1:T(8,128)(2,1)S(1)} %get-tuple-element.16), channel_id=1, source_target_pairs={{0,1},{1,2},{2,3},{4,5},{5,6},{6,7},{8,9},{9,10},{10,11},{12,13},{... | collective-permute-start | bytes 1474568 | tf_op jit(solution)/shard_map/ppermute | solution.py:18
  131.2 19.6 %collective-permute-start = (bf16[768,5,64]{0,2,1:T(8,128)(2,1)S(1)}, bf16[768,5,64]{0,2,1:T(8,128)(2,1)}, u32[]{:S(2)}, u32[]{:S(2)}) collective-permute-start(bf16[768,5,64]{0,2,1:T(8,128)(2,1)S(1)} %fusion.26), channel_id=1, source_target_pairs={{0,1},{1,2},{2,3},{4,5},{5,6},{6,7},{8,9},{9,10},{10,11},{12,13},{... | collective-permute-start | bytes 1474568 | tf_op jit(solution)/shard_map/ppermute | solution.py:18
  167.4 150.3 %all-gather.12.cloned.1.call-start = ((), (), s32[]{:S(2)}) async-start(), calls=%async_computation.6 | async-start | bytes 7372800 | tf_op jit(solution)/shard_map/all_gather | solution.py:148
  170.4 169.7 %all-gather.10.cloned.1.call-start = ((), (), s32[]{:S(2)}) async-start(), calls=%async_computation.5 | async-start | bytes 2457600 | tf_op jit(solution)/shard_map/all_gather | solution.py:147
  173.5 55.7 %copy-start.8 = (f32[1280]{0:T(1024)S(1)}, f32[1280]{0:T(1024)}, u32[]{:S(2)}) copy-start(f32[1280]{0:T(1024)} %get-tuple-element.9) | copy-start | bytes 15364
  173.5 55.7 %copy-start.1 = (f32[1280,160]{0,1:T(8,128)S(1)}, f32[1280,160]{0,1:T(8,128)}, u32[]{:S(2)}) copy-start(f32[1280,160]{0,1:T(8,128)} %param.15) | copy-start | bytes 2457604
  229.2 173.8 %all-gather.14.cloned.1.call-start = ((), (), s32[]{:S(2)}) async-start(), calls=%async_computation.7 | async-start | bytes 3686400 | tf_op jit(solution)/shard_map/all_gather | solution.py:152
  230.1 224.5 %reduce-scatter.5.cloned.1.call-start = ((), (), s32[]{:S(2)}) async-start(), calls=%async_computation.8 | async-start | bytes 4915200 | tf_op jit(solution)/shard_map/reduce_scatter | solution.py:153
  340.1 62.9 %copy-start.10 = (f32[1280]{0:T(1024)S(1)}, f32[1280]{0:T(1024)}, u32[]{:S(2)}) copy-start(f32[1280]{0:T(1024)} %param.20) | copy-start | bytes 15364
  340.1 62.9 %copy-start.11 = (f32[1280]{0:T(1024)S(1)}, f32[1280]{0:T(1024)}, u32[]{:S(2)}) copy-start(f32[1280]{0:T(1024)} %param.19) | copy-start | bytes 15364
Sparse Core Ops, SparseCore 0:
  8.9 24.3 all-gather.5
  45.7 71.1 all-gather.7
  167.5 46.1 reduce-scatter.2
  215.8 101.8 all-gather.11
  319.2 20.7 all-gather.9
  342.2 60.6 all-gather.13
  412.2 42.3 reduce-scatter.4
where the time goes:
time: 486 us; the launch traced here: 479 us
  waiting for transfers between devices  269 us (55%)
  blocking collectives  89.8 us (18%)
  matrix products  49.7 us (10%)
  other arithmetic  32.1 us (7%)
  local copies, waits for them, and re-layouts  14.7 us (3%)
  between operations  14.2 us (3%)
  starting transfers between devices  9.05 us (2%)
    all_gather x1, waiting for transfers between devices, body(): lax.all_gather(gate_up_norm, ('rep', 'cp'), axis=0, tiled=True)  87.4 us
    all_gather x1, waiting for transfers between devices, body(): lax.all_gather(down_norm, ('rep', 'cp'), axis=1, tiled=True)  52.3 us
    reduce_scatter x1, waiting for transfers between devices, body(): lax.psum_scatter(mlp_part, 'tp', scatter_dimension=1, tiled=True)  41.7 us
    reduce_scatter x1, waiting for transfers between devices, body(): lax.psum_scatter(attn_part, 'tp', scatter_dimension=1, tiled=True)  40.2 us
    all_gather x1, blocking collectives, body(): lax.all_gather(out_norm, ('rep', 'cp'), axis=1, tiled=True)  34.9 us
    psum x1, blocking collectives, body(): lax.psum((jnp.sum(qkv_weight * qkv_weight, axis=0), jnp.sum(out_weight *...  31.9 us
    all_gather x1, waiting for transfers between devices, body(): lax.all_gather(qkv_norm, ('rep', 'cp'), axis=0, tiled=True)  27.5 us
    psum x4, blocking collectives, share_unit(): totals = lax.psum(jnp.sum(array * array, axis=-1), 'tp')  23 us
  transfers between devices with their start and end apart: 9, of which 7 were waited for; matrix products, arithmetic and copies ran while one was open for 12% of the time, Pallas kernels for 0%

commit v1 on v0

--- a/solution.py
+++ b/solution.py
@@ -3,6 +3,8 @@
 import jax
 import jax.numpy as jnp
 from jax import lax
+from jax.experimental import pallas as pl
+from jax.experimental.pallas import tpu as pltpu
 from jax.sharding import PartitionSpec as P
 
 D = 1280
@@ -61,7 +63,7 @@
     return jnp.dot(left, piece, preferred_element_type=jnp.float32)
 
 
-def body(
+def plain_body(
     tokens,
     qkv_weight,
     out_weight,
@@ -155,6 +157,416 @@
     result = math.sqrt(D) * share_unit(mixed + mlp_rate_block * (share_unit(mlp_block) - mixed))
     return result.astype(jnp.bfloat16)[None]
 
+MESH = pl.DeviceIdType.MESH
+PARTS = 5
+BACK = 512
+NT = (((1,), (1,)), ((), ()))
+
+
+def column_scale(block_ref, shards):
+    def add(i, total):
+        piece = block_ref[i].astype(jnp.float32)
+        return total + jnp.sum(piece * piece, axis=0, keepdims=True)
+
+    zero = jnp.zeros((1, block_ref.shape[-1]), jnp.float32)
+    return lax.rsqrt(lax.fori_loop(0, shards, add, zero) + EPS)
+
+
+def fused_kernel(
+    reps, tps, cps,
+    tok_ref, wa_ref, wb_ref, cos_ref, sin_ref, start_ref, qks_ref, arate_ref, mrate_ref, ups_ref, gates_ref,
+    out_ref,
+    tok, xt, wa, wb, wo, csa, q_s, kv, sbuf, rbuf, xm, mix, macc, sbuf2, rbuf2, obuf, fin,
+    tok_send, tok_recv, w_send_z, w_send_y, w_recv, kv_send, kv_recv,
+    a_send, a_recv, m_send, m_recv, b_send, b_recv, o_send, o_recv,
+):
+    r, t, c = lax.axis_index("rep"), lax.axis_index("tp"), lax.axis_index("cp")
+    shards = reps * cps
+    tile = xt.shape[1]
+    width = xt.shape[2]
+    local = tok.shape[2]
+    heads = local // HD
+    depth = wa.shape[1]
+    hid = wb.shape[3] // 3
+    mine = r * cps + c
+
+    def tp_peer(d):
+        return lax.rem(t + d, tps)
+
+    def cp_peer(d):
+        return lax.rem(c + d, cps)
+
+    def rep_peer(d):
+        return lax.rem(r + d, reps)
+
+    barrier = pltpu.get_barrier_semaphore()
+    for d in range(1, tps):
+        pl.semaphore_signal(barrier, inc=1, device_id=(r, tp_peer(d), c), device_id_type=MESH)
+    for d in range(1, cps):
+        pl.semaphore_signal(barrier, inc=1, device_id=(r, t, cp_peer(d)), device_id_type=MESH)
+    for d in range(1, reps):
+        pl.semaphore_signal(barrier, inc=1, device_id=(rep_peer(d), t, c), device_id_type=MESH)
+    pl.semaphore_wait(barrier, tps + cps + reps - 3)
+
+    def remote(src, dst, send, recv, device):
+        return pltpu.make_async_remote_copy(
+            src_ref=src, dst_ref=dst, send_sem=send, recv_sem=recv, device_id=device, device_id_type=MESH
+        )
+
+    def slot(j, s):
+        return wa.at[s] if j is None else wb.at[j, s]
+
+    def own(j):
+        return wa_ref if j is None else wb_ref.at[j]
+
+    def row(j):
+        return 0 if j is None else j + 1
+
+    def z_copy(j, d):
+        return remote(own(j), slot(j, mine), w_send_z.at[row(j), d], w_recv.at[row(j), mine], (r, t, cp_peer(d)))
+
+    def y_copy(j, k, d):
+        s = r * cps + cp_peer(k)
+        source = own(j) if k == 0 else slot(j, s)
+        return remote(source, slot(j, s), w_send_y.at[row(j), k, d], w_recv.at[row(j), s], (rep_peer(d), t, c))
+
+    def arrive(j, s):
+        remote(own(j), slot(j, s), w_send_z.at[row(j), 0], w_recv.at[row(j), s], (r, t, cp_peer(1))).wait_recv()
+
+    def send_own(j):
+        for d in range(1, reps):
+            y_copy(j, 0, d).start()
+        for d in range(1, cps):
+            z_copy(j, d).start()
+
+    def comm_step(j, k):
+        arrive(j, r * cps + cp_peer(k))
+        for d in range(1, reps):
+            y_copy(j, k, d).start()
+
+    def comm_part(j):
+        @pl.when(j + 1 < PARTS)
+        def _():
+            send_own(j + 1)
+
+        for k in range(1, cps):
+            comm_step(j, k)
+
+    def finish_part(j):
+        for d in range(1, reps):
+            for k in range(cps):
+                arrive(j, rep_peer(d) * cps + cp_peer(k))
+
+    def drain(j):
+        for d in range(1, cps):
+            z_copy(j, d).wait_send()
+        for d in range(1, reps):
+            for k in range(cps):
+                y_copy(j, k, d).wait_send()
+
+    def tok_copy(d):
+        return remote(tok_ref, tok.at[t], tok_send.at[d], tok_recv.at[t], (r, tp_peer(d), c))
+
+    for d in range(1, tps):
+        tok_copy(d).start()
+    send_own(None)
+    tok[t] = tok_ref[...]
+    wa[mine] = wa_ref[...]
+
+    @pl.loop(0, PARTS)
+    def _(j):
+        wb[j, mine] = wb_ref[j]
+
+    for d in range(1, tps):
+        s = tp_peer(d)
+        remote(tok_ref, tok.at[s], tok_send.at[d], tok_recv.at[s], (r, s, c)).wait_recv()
+    send_own(0)
+    for k in range(1, cps):
+        comm_step(None, k)
+    finish_part(None)
+    csa[...] = column_scale(wa, shards)
+    wo[...] = wa[:, :, 3 * local :].reshape(width, local)
+
+    def project(i, carry):
+        rows = pl.ds(pl.multiple_of(i * tile, 64), tile)
+        x = jnp.concatenate([tok[s, rows, :] for s in range(tps)], axis=1)
+        xt[i] = x
+        xf = x.astype(jnp.float32)
+        inv = lax.rsqrt(jnp.sum(xf * xf, axis=1, keepdims=True) + EPS)
+        weights = wa[:, :, : 3 * local].reshape(width, 3 * local)
+        pr = jnp.dot(x, weights, preferred_element_type=jnp.float32) * inv * csa[:, : 3 * local]
+        cosine, sine = cos_ref[i], sin_ref[i]
+
+        def rope(base, factor):
+            pieces = []
+            for h in range(heads):
+                v = pr[:, base + HD * h : base + HD * (h + 1)]
+                v = v * lax.rsqrt(jnp.sum(v * v, axis=1, keepdims=True) + EPS)
+                v = v * (qks_ref[:, HD * h : HD * (h + 1)] * factor)
+                swapped = jnp.concatenate([v[:, HD // 2 :], v[:, : HD // 2]], axis=1)
+                pieces.append(v * cosine + swapped * sine)
+            return jnp.concatenate(pieces, axis=1)
+
+        q_s[i] = rope(0, math.sqrt(HD)).astype(jnp.bfloat16)
+        kv[pl.ds(pl.multiple_of(BACK + i * tile, 64), tile), :] = jnp.concatenate(
+            [rope(local, 1.0), pr[:, 2 * local :]], axis=1
+        ).astype(jnp.bfloat16)
+        return carry
+
+    lax.fori_loop(0, tps, project, 0)
+
+    rows_all = kv.shape[0]
+
+    def kv_copy():
+        return remote(
+            kv.at[pl.ds(rows_all - BACK, BACK)], kv.at[pl.ds(0, BACK)], kv_send, kv_recv, (r, t, cp_peer(1))
+        )
+
+    @pl.when(c < cps - 1)
+    def _():
+        kv_copy().start()
+
+    @pl.when(c == 0)
+    def _():
+        kv[pl.ds(0, BACK), :] = jnp.zeros((BACK, kv.shape[1]), kv.dtype)
+
+    window = BACK + tile
+
+    def part_copy(sent, got, p, send, recv):
+        return remote(sent.at[p], got.at[t], send.at[p], recv.at[t], (r, p, c))
+
+    def attend(step, carry):
+        i = tps - 1 - step
+
+        @pl.when((step == 1) & (c > 0))
+        def _():
+            kv_copy().wait_recv()
+
+        first = pl.ds(pl.multiple_of(i * tile, 64), window)
+        column = lax.broadcasted_iota(jnp.int32, (tile, window), 1)
+        line = lax.broadcasted_iota(jnp.int32, (tile, window), 0) + BACK
+        allowed = (column <= line) & (column >= start_ref[i] - i * tile)
+        qt = q_s[i]
+        outs = []
+        for h in range(heads):
+            keys = kv[first, HD * h : HD * (h + 1)]
+            values = kv[first, local + HD * h : local + HD * (h + 1)]
+            scores = lax.dot_general(
+                qt[:, HD * h : HD * (h + 1)], keys, NT, preferred_element_type=jnp.float32
+            )
+            scores = jnp.where(allowed, scores, -1e30)
+            exponent = jnp.exp(scores - jnp.max(scores, axis=1, keepdims=True))
+            total = jnp.sum(exponent, axis=1, keepdims=True)
+            got = jnp.dot(exponent.astype(jnp.bfloat16), values, preferred_element_type=jnp.float32)
+            outs.append(got / total)
+        att = (jnp.concatenate(outs, axis=1) * csa[:, 3 * local :]).astype(jnp.bfloat16)
+        sbuf[i] = lax.dot_general(att, wo[...], NT, preferred_element_type=jnp.float32).astype(jnp.bfloat16)
+
+        @pl.when(i != t)
+        def _():
+            part_copy(sbuf, rbuf, i, a_send, a_recv).start()
+
+        @pl.when(i == t)
+        def _():
+            rbuf[t] = sbuf[t]
+
+        @pl.when(step < 3)
+        def _():
+            comm_part(step)
+
+        return carry
+
+    lax.fori_loop(0, tps, attend, 0)
+
+    def gather_parts(sent, got, send, recv):
+        for d in range(1, tps):
+            s = tp_peer(d)
+            remote(sent.at[t], got.at[s], send.at[t], recv.at[s], (r, s, c)).wait_recv()
+        total = got[0].astype(jnp.float32)
+        for s in range(1, tps):
+            total = total + got[s].astype(jnp.float32)
+        return total
+
+    def unit(v):
+        return v * lax.rsqrt(jnp.sum(v * v, axis=1, keepdims=True) + EPS)
+
+    attn = unit(gather_parts(sbuf, rbuf, a_send, a_recv))
+    state = unit(xt[t].astype(jnp.float32))
+    mixed = unit(state + arate_ref[...] * (attn - state))
+    mix[...] = mixed
+    xm[t] = mixed.astype(jnp.bfloat16)
+
+    def mix_copy(d):
+        return remote(xm.at[t], xm.at[t], m_send.at[d], m_recv.at[t], (r, tp_peer(d), c))
+
+    for d in range(1, tps):
+        mix_copy(d).start()
+    comm_part(3)
+    for d in range(1, tps):
+        s = tp_peer(d)
+        remote(xm.at[s], xm.at[s], m_send.at[d], m_recv.at[s], (r, s, c)).wait_recv()
+
+    def feed(j, carry):
+        finish_part(j)
+        cs = column_scale(wb.at[j], shards)
+        up_by = cs[:, :hid] * ups_ref[j]
+        gate_by = cs[:, hid : 2 * hid] * gates_ref[j] * math.sqrt(width)
+        down_by = cs[:, 2 * hid :]
+
+        def one(step, inner_carry):
+            p = tp_peer(step + 1)
+            gu = jnp.dot(
+                xm[p], wb[j, :, :, : 2 * hid].reshape(width, 2 * hid), preferred_element_type=jnp.float32
+            )
+            up = gu[:, :hid] * up_by
+            gate = gu[:, hid:] * gate_by
+            inner = (up * (gate / (1.0 + jnp.exp(-gate))) * down_by).astype(jnp.bfloat16)
+            part = lax.dot_general(
+                inner, wb[j, :, :, 2 * hid :].reshape(width, hid), NT, preferred_element_type=jnp.float32
+            )
+
+            @pl.when(j == 0)
+            def _():
+                macc[p] = part
+
+            @pl.when((j > 0) & (j < PARTS - 1))
+            def _():
+                macc[p] = macc[p] + part
+
+            @pl.when(j == PARTS - 1)
+            def _():
+                sbuf2[p] = (macc[p] + part).astype(jnp.bfloat16)
+
+            @pl.when((j == PARTS - 1) & (p != t))
+            def _():
+                part_copy(sbuf2, rbuf2, p, b_send, b_recv).start()
+
+            return inner_carry
+
+        lax.fori_loop(0, tps, one, 0)
+
+        @pl.when(j == 0)
+        def _():
+            comm_part(4)
+
+        return carry
+
+    lax.fori_loop(0, PARTS, feed, 0)
+    rbuf2[t] = sbuf2[t]
+    mlp = unit(gather_parts(sbuf2, rbuf2, b_send, b_recv))
+    kept = mix[...]
+    final = (math.sqrt(width) * unit(kept + mrate_ref[...] * (mlp - kept))).astype(jnp.bfloat16)
+    for p in range(tps):
+        obuf[p] = final[:, local * p : local * (p + 1)]
+
+    def out_copy(p):
+        return remote(obuf.at[p], fin.at[t], o_send.at[p], o_recv.at[t], (r, p, c))
+
+    for d in range(1, tps):
+        out_copy(tp_peer(d)).start()
+    fin[t] = obuf[t]
+    for d in range(1, tps):
+        s = tp_peer(d)
+        remote(obuf.at[t], fin.at[s], o_send.at[t], o_recv.at[s], (r, s, c)).wait_recv()
+    for s in range(tps):
+        out_ref[pl.ds(s * tile, tile), :] = fin[s]
+
+    drain(None)
+
+    @pl.loop(0, PARTS)
+    def _(j):
+        drain(j)
+
+    for d in range(1, tps):
+        p = tp_peer(d)
+        tok_copy(d).wait_send()
+        part_copy(sbuf, rbuf, p, a_send, a_recv).wait_send()
+        mix_copy(d).wait_send()
+        part_copy(sbuf2, rbuf2, p, b_send, b_recv).wait_send()
+        out_copy(p).wait_send()
+
+    @pl.when(c < cps - 1)
+    def _():
+        kv_copy().wait_send()
+
+
+def fused_body(
+    tokens, qkv_weight, out_weight, gate_up_weight, down_weight, qk_scale,
+    attn_rate, mlp_rate, up_scale, gate_scale, segment_ids,
+):
+    reps, tps, cps = lax.axis_size("rep"), lax.axis_size("tp"), lax.axis_size("cp")
+    rows, local = tokens.shape[1], tokens.shape[2]
+    depth = qkv_weight.shape[0]
+    hidden = gate_up_weight.shape[2]
+    hid = hidden // PARTS
+    shards = reps * cps
+    width = depth * shards
+    tile = rows // tps
+    bf16 = jnp.bfloat16
+    wa = jnp.concatenate(
+        [qkv_weight.reshape(depth, 3 * local).astype(bf16), out_weight.astype(bf16).T], axis=1
+    )
+    gu = gate_up_weight.astype(bf16).reshape(depth, 2, PARTS, hid).transpose(2, 0, 1, 3)
+    down = down_weight.astype(bf16).reshape(PARTS, hid, depth).transpose(0, 2, 1)
+    wb = jnp.concatenate([gu.reshape(PARTS, depth, 2 * hid), down], axis=2)
+    position = stream_positions(segment_ids[0])
+    own_pos = lax.dynamic_slice_in_dim(position, lax.axis_index("cp") * rows, rows)
+    half = HD // 2
+    frequency = jnp.exp(-math.log(10000.0) * jnp.arange(half, dtype=jnp.float32) * 2.0 / HD)
+    angles = own_pos.astype(jnp.float32)[:, None] * frequency[None, :]
+    cosine, sine = jnp.cos(angles), jnp.sin(angles)
+    cos_table = jnp.concatenate([cosine, cosine], axis=1).reshape(tps, tile, HD)
+    sin_table = jnp.concatenate([-sine, sine], axis=1).reshape(tps, tile, HD)
+    starts = (BACK + jnp.arange(rows, dtype=jnp.int32) - own_pos).reshape(tps, tile, 1)
+    vmem = pl.BlockSpec(memory_space=pltpu.VMEM)
+    dma = pltpu.SemaphoreType.DMA
+    f32 = jnp.float32
+    flops = 2 * rows * width * (4 * local + 3 * hidden) + 4 * rows * (BACK + tile) * local
+    out = pl.pallas_call(
+        lambda *refs: fused_kernel(reps, tps, cps, *refs),
+        out_shape=jax.ShapeDtypeStruct((rows, local), bf16),
+        in_specs=[vmem] * 11,
+        out_specs=vmem,
+        scratch_shapes=[
+            pltpu.VMEM((tps, rows, local), bf16),
+            pltpu.VMEM((tps, tile, width), bf16),
+            pltpu.VMEM((shards, depth, 4 * local), bf16),
+            pltpu.VMEM((PARTS, shards, depth, 3 * hid), bf16),
+            pltpu.VMEM((width, local), bf16),
+            pltpu.VMEM((1, 4 * local), f32),
+            pltpu.VMEM((tps, tile, local), bf16),
+            pltpu.VMEM((BACK + rows, 2 * local), bf16),
+            pltpu.VMEM((tps, tile, width), bf16),
+            pltpu.VMEM((tps, tile, width), bf16),
+            pltpu.VMEM((tps, tile, width), bf16),
+            pltpu.VMEM((tile, width), f32),
+            pltpu.VMEM((tps, tile, width), f32),
+            pltpu.VMEM((tps, tile, width), bf16),
+            pltpu.VMEM((tps, tile, width), bf16),
+            pltpu.VMEM((tps, tile, local), bf16),
+            pltpu.VMEM((tps, tile, local), bf16),
+            dma((tps,)), dma((tps,)),
+            dma((PARTS + 1, cps)), dma((PARTS + 1, cps, reps)), dma((PARTS + 1, shards)),
+            dma, dma,
+            dma((tps,)), dma((tps,)), dma((tps,)), dma((tps,)),
+            dma((tps,)), dma((tps,)), dma((tps,)), dma((tps,)),
+        ],
+        compiler_params=pltpu.CompilerParams(
+            collective_id=0, has_side_effects=True, vmem_limit_bytes=58 * 1024 * 1024
+        ),
+        cost_estimate=pl.CostEstimate(flops=flops, bytes_accessed=2 * width * 5120, transcendentals=0),
+    )(
+        tokens[0], wa, wb, cos_table, sin_table, starts, qk_scale[None], attn_rate[None], mlp_rate[None],
+        up_scale.reshape(PARTS, 1, hid), gate_scale.reshape(PARTS, 1, hid),
+    )
+    return out[None]
+
+
+def body(*arrays):
+    depth, tile = arrays[1].shape[0], arrays[0].shape[1] // lax.axis_size("tp")
+    aligned = depth % 16 == 0 and tile % 64 == 0 and arrays[3].shape[2] % (128 * PARTS) == 0
+    return fused_body(*arrays) if aligned else plain_body(*arrays)
+
 
 def solution(mesh):
     in_specs = (

time: 486 us -> 272 us (0.56)
  the two profiles are of different devices: /device:TPU:1 before, /device:TPU:17 now
where the time goes in v1:
time: 272 us; the launch traced here: 271 us
  Pallas kernels  251 us (92%)
  local copies, waits for them, and re-layouts  12.8 us (5%)
  other arithmetic  7.26 us (3%)
    pallas_call x1, Pallas kernels, fused_body(): pl.pallas_call(lambda *refs: fused_kernel(reps, tps, cps, *refs), out_sha...  251 us

profile of v1, /device:TPU:17, one launch (start us, length us, event | category | flops | bytes accessed | tf_op | source)
XLA Modules:
  0.0 271.2 jit_solution(163551102775146804)
XLA Ops:
  0.0 1.2 slice.19
  1.2 1.5 add_select_fusion
  2.7 0.3 reduce-window.9
  3.4 1.5 fusion
  4.9 1.2 pad_maximum_fusion.2
  6.1 1.0 reshape.94.refs_5_
  7.1 0.6 convert_element_type.21
  7.8 0.9 reshape.87
  8.7 0.9 copy.19
  9.6 0.5 reshape.88
  10.2 0.6 copy-done.1
  10.9 1.1 pad_maximum_fusion.refs_2_
  12.3 0.3 copy.17
  12.6 0.3 convert_element_type.19
  12.9 0.3 copy-done.4
  13.2 0.9 pad_maximum_fusion.1.refs_1_
  14.1 1.1 copy.16
  15.2 0.6 broadcast_in_dim.19.refs_7_
  15.8 0.6 broadcast_in_dim.20.refs_8_
  16.4 0.6 reshape.92.refs_9_
  17.0 0.6 reshape.93.refs_10_
  17.6 0.6 broadcast_in_dim.18.refs_6_
  18.2 250.9 %shard_map.109 = bf16[768,320]{1,0:T(8,128)(2,1)} custom-call(bf16[768,320]{1,0:T(8,128)(2,1)} %bitcast.30, bf16[160,1280]{1,0:T(8,128)(2,1)} %pad_maximum_fusion.1.refs_1_, bf16[5,160,768]{2,1,0:T(8,128)(2,1)} %pad_maximum_fusion.refs_2_, f32[4,192,64]{2,1,0:T(8,128)} %get-tuple-element.10.refs_3_, f32[4,192,64]{2,1,0:T(8,128)} %get-tuple-element.11.refs_4_, ...), custom_call_target="tpu_custom_call" | custom-call | flops 10758389760 | bytes 13107200 | tf_op jit(solution)/shard_map/pallas_call | solution.py:525
  269.1 2.1 copy.22
  (30 shorter events, 1.0 us)
Async XLA Ops:
  4.9 2.2 copy-start
  9.6 1.1 copy-start.1
  10.8 1.4 copy-start.2
  12.2 0.9 copy-start.4
  12.3 1.8 copy-start.3
  13.2 2.0 copy-start.5
  13.2 2.6 copy-start.6
  13.2 3.2 %copy-start.7 = (f32[1280]{0:T(1024)S(1)}, f32[1280]{0:T(1024)}, u32[]{:S(2)}) copy-start(f32[1280]{0:T(1024)} %param.19) | copy-start | bytes 15364
  13.2 3.8 %copy-start.8 = (f32[1280]{0:T(1024)S(1)}, f32[1280]{0:T(1024)}, u32[]{:S(2)}) copy-start(f32[1280]{0:T(1024)} %param.20) | copy-start | bytes 15364
  13.2 4.4 %copy-start.9 = (f32[320]{0:T(512)S(1)}, f32[320]{0:T(512)}, u32[]{:S(2)}) copy-start(f32[320]{0:T(512)} %param.16) | copy-start | bytes 3844

commit v2 on v1

--- a/solution.py
+++ b/solution.py
@@ -174,9 +174,9 @@
 
 def fused_kernel(
     reps, tps, cps,
-    tok_ref, wa_ref, wb_ref, cos_ref, sin_ref, start_ref, qks_ref, arate_ref, mrate_ref, ups_ref, gates_ref,
-    out_ref,
-    tok, xt, wa, wb, wo, csa, q_s, kv, sbuf, rbuf, xm, mix, macc, sbuf2, rbuf2, obuf, fin,
+    tok_all, wa_ref, wb_ref, table_ref, vec_ref,
+    out_all,
+    tok, xt, wa, wb, wo, csa, q_s, kv, near, far, xm, mix, macc, kept_part, near2, far2, obuf, fin,
     tok_send, tok_recv, w_send_z, w_send_y, w_recv, kv_send, kv_recv,
     a_send, a_recv, m_send, m_recv, b_send, b_recv, o_send, o_recv,
 ):
@@ -189,6 +189,11 @@
     depth = wa.shape[1]
     hid = wb.shape[3] // 3
     mine = r * cps + c
+    hidden = PARTS * hid
+    tok_ref, out_ref = tok_all.at[0], out_all.at[0]
+    beside = t + 1 - 2 * lax.rem(t, 2)
+    across = lax.rem(t + 2, tps)
+    diagonal = lax.rem(beside + 2, tps)
 
     def tp_peer(d):
         return lax.rem(t + d, tps)
@@ -245,9 +250,9 @@
             y_copy(j, k, d).start()
 
     def comm_part(j):
-        @pl.when(j + 1 < PARTS)
-        def _():
-            send_own(j + 1)
+        @pl.when(j + 2 < PARTS)
+        def _():
+            send_own(j + 2)
 
         for k in range(1, cps):
             comm_step(j, k)
@@ -280,14 +285,24 @@
     for d in range(1, tps):
         s = tp_peer(d)
         remote(tok_ref, tok.at[s], tok_send.at[d], tok_recv.at[s], (r, s, c)).wait_recv()
-    send_own(0)
     for k in range(1, cps):
         comm_step(None, k)
+    send_own(0)
     finish_part(None)
+    send_own(1)
     csa[...] = column_scale(wa, shards)
     wo[...] = wa[:, :, 3 * local :].reshape(width, local)
 
-    def project(i, carry):
+    qks_at = 2 * width + 2 * hidden
+    rows_all = kv.shape[0]
+
+    def kv_copy():
+        return remote(
+            kv.at[pl.ds(rows_all - BACK, BACK)], kv.at[pl.ds(0, BACK)], kv_send, kv_recv, (r, t, cp_peer(1))
+        )
+
+    def project(step, carry):
+        i = tps - 1 - step
         rows = pl.ds(pl.multiple_of(i * tile, 64), tile)
         x = jnp.concatenate([tok[s, rows, :] for s in range(tps)], axis=1)
         xt[i] = x
@@ -295,14 +310,14 @@
         inv = lax.rsqrt(jnp.sum(xf * xf, axis=1, keepdims=True) + EPS)
         weights = wa[:, :, : 3 * local].reshape(width, 3 * local)
         pr = jnp.dot(x, weights, preferred_element_type=jnp.float32) * inv * csa[:, : 3 * local]
-        cosine, sine = cos_ref[i], sin_ref[i]
+        cosine, sine = table_ref[i, :, :HD], table_ref[i, :, HD : 2 * HD]
 
         def rope(base, factor):
             pieces = []
             for h in range(heads):
                 v = pr[:, base + HD * h : base + HD * (h + 1)]
                 v = v * lax.rsqrt(jnp.sum(v * v, axis=1, keepdims=True) + EPS)
-                v = v * (qks_ref[:, HD * h : HD * (h + 1)] * factor)
+                v = v * (vec_ref[:, qks_at + HD * h : qks_at + HD * (h + 1)] * factor)
                 swapped = jnp.concatenate([v[:, HD // 2 :], v[:, : HD // 2]], axis=1)
                 pieces.append(v * cosine + swapped * sine)
             return jnp.concatenate(pieces, axis=1)
@@ -311,41 +326,72 @@
         kv[pl.ds(pl.multiple_of(BACK + i * tile, 64), tile), :] = jnp.concatenate(
             [rope(local, 1.0), pr[:, 2 * local :]], axis=1
         ).astype(jnp.bfloat16)
+
+        @pl.when((step == (BACK - 1) // tile) & (c < cps - 1))
+        def _():
+            kv_copy().start()
+
         return carry
-
-    lax.fori_loop(0, tps, project, 0)
-
-    rows_all = kv.shape[0]
-
-    def kv_copy():
-        return remote(
-            kv.at[pl.ds(rows_all - BACK, BACK)], kv.at[pl.ds(0, BACK)], kv_send, kv_recv, (r, t, cp_peer(1))
-        )
-
-    @pl.when(c < cps - 1)
-    def _():
-        kv_copy().start()
 
     @pl.when(c == 0)
     def _():
         kv[pl.ds(0, BACK), :] = jnp.zeros((BACK, kv.shape[1]), kv.dtype)
 
+    lax.fori_loop(0, tps, project, 0)
+
+    @pl.when(c > 0)
+    def _():
+        kv_copy().wait_recv()
+
     window = BACK + tile
 
-    def part_copy(sent, got, p, send, recv):
-        return remote(sent.at[p], got.at[t], send.at[p], recv.at[t], (r, p, c))
+    def near_copy(buf, k, send, recv):
+        return remote(buf.at[k], buf.at[2 + k], send.at[k], recv.at[k], (r, beside, c))
+
+    def far_copy(buf, send, recv):
+        return remote(buf.at[0], buf.at[1], send.at[2], recv.at[2], (r, across, c))
+
+    def scatter_step(step, part, kept, buf_near, buf_far, send, recv):
+        @pl.when(step == 0)
+        def _():
+            buf_near[0] = part.astype(jnp.bfloat16)
+            near_copy(buf_near, 0, send, recv).start()
+
+        @pl.when(step == 1)
+        def _():
+            near_copy(buf_near, 0, send, recv).wait_recv()
+            buf_far[0] = (part + buf_near[2].astype(jnp.float32)).astype(jnp.bfloat16)
+            far_copy(buf_far, send, recv).start()
+
+        @pl.when(step == 2)
+        def _():
+            buf_near[1] = part.astype(jnp.bfloat16)
+            near_copy(buf_near, 1, send, recv).start()
+
+        @pl.when(step == 3)
+        def _():
+            kept[...] = part
+
+    def scatter_total(kept, buf_near, buf_far, send, recv):
+        near_copy(buf_near, 1, send, recv).wait_recv()
+        far_copy(buf_far, send, recv).wait_recv()
+        return kept[...] + buf_near[3].astype(jnp.float32) + buf_far[1].astype(jnp.float32)
+
+    def scatter_drain(buf_near, buf_far, send, recv):
+        near_copy(buf_near, 0, send, recv).wait_send()
+        near_copy(buf_near, 1, send, recv).wait_send()
+        far_copy(buf_far, send, recv).wait_send()
+
+    def target(step):
+        late = jnp.where(step == 2, beside, t)
+        return jnp.where(step == 0, diagonal, jnp.where(step == 1, across, late))
 
     def attend(step, carry):
-        i = tps - 1 - step
-
-        @pl.when((step == 1) & (c > 0))
-        def _():
-            kv_copy().wait_recv()
-
+        i = target(step)
         first = pl.ds(pl.multiple_of(i * tile, 64), window)
         column = lax.broadcasted_iota(jnp.int32, (tile, window), 1)
         line = lax.broadcasted_iota(jnp.int32, (tile, window), 0) + BACK
-        allowed = (column <= line) & (column >= start_ref[i] - i * tile)
+        allowed = (column <= line) & (column >= table_ref[i, :, 2 * HD : 2 * HD + 1].astype(jnp.int32) - i * tile)
         qt = q_s[i]
         outs = []
         for h in range(heads):
@@ -360,90 +406,67 @@
             got = jnp.dot(exponent.astype(jnp.bfloat16), values, preferred_element_type=jnp.float32)
             outs.append(got / total)
         att = (jnp.concatenate(outs, axis=1) * csa[:, 3 * local :]).astype(jnp.bfloat16)
-        sbuf[i] = lax.dot_general(att, wo[...], NT, preferred_element_type=jnp.float32).astype(jnp.bfloat16)
-
-        @pl.when(i != t)
-        def _():
-            part_copy(sbuf, rbuf, i, a_send, a_recv).start()
-
-        @pl.when(i == t)
-        def _():
-            rbuf[t] = sbuf[t]
-
-        @pl.when(step < 3)
-        def _():
-            comm_part(step)
+        part = lax.dot_general(att, wo[...], NT, preferred_element_type=jnp.float32)
+        scatter_step(step, part, mix, near, far, a_send, a_recv)
+
+        @pl.when(lax.rem(step, 2) == 0)
+        def _():
+            comm_part(step // 2)
 
         return carry
 
     lax.fori_loop(0, tps, attend, 0)
-
-    def gather_parts(sent, got, send, recv):
-        for d in range(1, tps):
-            s = tp_peer(d)
-            remote(sent.at[t], got.at[s], send.at[t], recv.at[s], (r, s, c)).wait_recv()
-        total = got[0].astype(jnp.float32)
-        for s in range(1, tps):
-            total = total + got[s].astype(jnp.float32)
-        return total
 
     def unit(v):
         return v * lax.rsqrt(jnp.sum(v * v, axis=1, keepdims=True) + EPS)
 
-    attn = unit(gather_parts(sbuf, rbuf, a_send, a_recv))
+    attn = unit(scatter_total(mix, near, far, a_send, a_recv))
     state = unit(xt[t].astype(jnp.float32))
-    mixed = unit(state + arate_ref[...] * (attn - state))
+    mixed = unit(state + vec_ref[:, :width] * (attn - state))
     mix[...] = mixed
     xm[t] = mixed.astype(jnp.bfloat16)
 
-    def mix_copy(d):
-        return remote(xm.at[t], xm.at[t], m_send.at[d], m_recv.at[t], (r, tp_peer(d), c))
-
-    for d in range(1, tps):
-        mix_copy(d).start()
+    def mix_copy(k, s, device):
+        return remote(xm.at[s], xm.at[s], m_send.at[k], m_recv.at[s], (r, device, c))
+
+    mix_copy(0, t, across).start()
+    mix_copy(1, t, beside).start()
+    macc[...] = jnp.zeros_like(macc)
+    comm_part(2)
+    mix_copy(0, across, across).wait_recv()
+    mix_copy(2, across, beside).start()
+    mix_copy(1, beside, beside).wait_recv()
+    mix_copy(2, diagonal, beside).wait_recv()
     comm_part(3)
-    for d in range(1, tps):
-        s = tp_peer(d)
-        remote(xm.at[s], xm.at[s], m_send.at[d], m_recv.at[s], (r, s, c)).wait_recv()
-
-    def feed(j, carry):
+
+    def scales(j):
+        cs = column_scale(wb.at[j], shards)
+        mine_up = pl.ds(pl.multiple_of(2 * width + j * hid, 128), hid)
+        mine_gate = pl.ds(pl.multiple_of(2 * width + hidden + j * hid, 128), hid)
+        up_by = cs[:, :hid] * vec_ref[:, mine_up]
+        gate_by = cs[:, hid : 2 * hid] * vec_ref[:, mine_gate] * math.sqrt(width)
+        return up_by, gate_by, cs[:, 2 * hid :]
+
+    def feed(x, j, by):
+        gu = jnp.dot(x, wb[j, :, :, : 2 * hid].reshape(width, 2 * hid), preferred_element_type=jnp.float32)
+        up = gu[:, :hid] * by[0]
+        gate = gu[:, hid:] * by[1]
+        inner = (up * (gate / (1.0 + jnp.exp(-gate))) * by[2]).astype(jnp.bfloat16)
+        return lax.dot_general(
+            inner, wb[j, :, :, 2 * hid :].reshape(width, hid), NT, preferred_element_type=jnp.float32
+        )
+
+    def feed_part(j, carry):
         finish_part(j)
-        cs = column_scale(wb.at[j], shards)
-        up_by = cs[:, :hid] * ups_ref[j]
-        gate_by = cs[:, hid : 2 * hid] * gates_ref[j] * math.sqrt(width)
-        down_by = cs[:, 2 * hid :]
-
-        def one(step, inner_carry):
-            p = tp_peer(step + 1)
-            gu = jnp.dot(
-                xm[p], wb[j, :, :, : 2 * hid].reshape(width, 2 * hid), preferred_element_type=jnp.float32
-            )
-            up = gu[:, :hid] * up_by
-            gate = gu[:, hid:] * gate_by
-            inner = (up * (gate / (1.0 + jnp.exp(-gate))) * down_by).astype(jnp.bfloat16)
-            part = lax.dot_general(
-                inner, wb[j, :, :, 2 * hid :].reshape(width, hid), NT, preferred_element_type=jnp.float32
-            )
-
-            @pl.when(j == 0)
-            def _():
-                macc[p] = part
-
-            @pl.when((j > 0) & (j < PARTS - 1))
-            def _():
-                macc[p] = macc[p] + part
-
-            @pl.when(j == PARTS - 1)
-            def _():
-                sbuf2[p] = (macc[p] + part).astype(jnp.bfloat16)
-
-            @pl.when((j == PARTS - 1) & (p != t))
-            def _():
-                part_copy(sbuf2, rbuf2, p, b_send, b_recv).start()
-
+        by = scales(j)
+
+        def pair(i, inner_carry):
+            both = pl.ds(2 * i, 2)
+            part = feed(xm[both].reshape(2 * tile, width), j, by)
+            macc[both] = macc[both] + part.reshape(2, tile, width)
             return inner_carry
 
-        lax.fori_loop(0, tps, one, 0)
+        lax.fori_loop(0, tps // 2, pair, 0)
 
         @pl.when(j == 0)
         def _():
@@ -451,11 +474,20 @@
 
         return carry
 
-    lax.fori_loop(0, PARTS, feed, 0)
-    rbuf2[t] = sbuf2[t]
-    mlp = unit(gather_parts(sbuf2, rbuf2, b_send, b_recv))
+    lax.fori_loop(0, PARTS - 1, feed_part, 0)
+    finish_part(PARTS - 1)
+    last_by = scales(PARTS - 1)
+
+    def feed_last(step, carry):
+        p = target(step)
+        part = macc[p] + feed(xm[p], PARTS - 1, last_by)
+        scatter_step(step, part, kept_part, near2, far2, b_send, b_recv)
+        return carry
+
+    lax.fori_loop(0, tps, feed_last, 0)
+    mlp = unit(scatter_total(kept_part, near2, far2, b_send, b_recv))
     kept = mix[...]
-    final = (math.sqrt(width) * unit(kept + mrate_ref[...] * (mlp - kept))).astype(jnp.bfloat16)
+    final = (math.sqrt(width) * unit(kept + vec_ref[:, width : 2 * width] * (mlp - kept))).astype(jnp.bfloat16)
     for p in range(tps):
         obuf[p] = final[:, local * p : local * (p + 1)]
 
@@ -480,10 +512,13 @@
     for d in range(1, tps):
         p = tp_peer(d)
         tok_copy(d).wait_send()
-        part_copy(sbuf, rbuf, p, a_send, a_recv).wait_send()
-        mix_copy(d).wait_send()
-        part_copy(sbuf2, rbuf2, p, b_send, b_recv).wait_send()
         out_copy(p).wait_send()
+
+    scatter_drain(near, far, a_send, a_recv)
+    scatter_drain(near2, far2, b_send, b_recv)
+    mix_copy(0, t, across).wait_send()
+    mix_copy(1, t, beside).wait_send()
+    mix_copy(2, across, beside).wait_send()
 
     @pl.when(c < cps - 1)
     def _():
@@ -515,17 +550,19 @@
     frequency = jnp.exp(-math.log(10000.0) * jnp.arange(half, dtype=jnp.float32) * 2.0 / HD)
     angles = own_pos.astype(jnp.float32)[:, None] * frequency[None, :]
     cosine, sine = jnp.cos(angles), jnp.sin(angles)
-    cos_table = jnp.concatenate([cosine, cosine], axis=1).reshape(tps, tile, HD)
-    sin_table = jnp.concatenate([-sine, sine], axis=1).reshape(tps, tile, HD)
-    starts = (BACK + jnp.arange(rows, dtype=jnp.int32) - own_pos).reshape(tps, tile, 1)
+    first = (BACK + jnp.arange(rows, dtype=jnp.int32) - own_pos).astype(jnp.float32)[:, None]
+    table = jnp.concatenate(
+        [cosine, cosine, -sine, sine, jnp.broadcast_to(first, (rows, 2 * HD))], axis=1
+    ).reshape(tps, tile, 4 * HD)
+    vectors = jnp.concatenate([attn_rate, mlp_rate, up_scale, gate_scale, qk_scale])[None]
     vmem = pl.BlockSpec(memory_space=pltpu.VMEM)
     dma = pltpu.SemaphoreType.DMA
     f32 = jnp.float32
     flops = 2 * rows * width * (4 * local + 3 * hidden) + 4 * rows * (BACK + tile) * local
     out = pl.pallas_call(
         lambda *refs: fused_kernel(reps, tps, cps, *refs),
-        out_shape=jax.ShapeDtypeStruct((rows, local), bf16),
-        in_specs=[vmem] * 11,
+        out_shape=jax.ShapeDtypeStruct((1, rows, local), bf16),
+        in_specs=[vmem] * 5,
         out_specs=vmem,
         scratch_shapes=[
             pltpu.VMEM((tps, rows, local), bf16),
@@ -536,13 +573,14 @@
             pltpu.VMEM((1, 4 * local), f32),
             pltpu.VMEM((tps, tile, local), bf16),
             pltpu.VMEM((BACK + rows, 2 * local), bf16),
-            pltpu.VMEM((tps, tile, width), bf16),
-            pltpu.VMEM((tps, tile, width), bf16),
+            pltpu.VMEM((4, tile, width), bf16),
+            pltpu.VMEM((2, tile, width), bf16),
             pltpu.VMEM((tps, tile, width), bf16),
             pltpu.VMEM((tile, width), f32),
             pltpu.VMEM((tps, tile, width), f32),
-            pltpu.VMEM((tps, tile, width), bf16),
-            pltpu.VMEM((tps, tile, width), bf16),
+            pltpu.VMEM((tile, width), f32),
+            pltpu.VMEM((4, tile, width), bf16),
+            pltpu.VMEM((2, tile, width), bf16),
             pltpu.VMEM((tps, tile, local), bf16),
             pltpu.VMEM((tps, tile, local), bf16),
             dma((tps,)), dma((tps,)),
@@ -556,15 +594,14 @@
         ),
         cost_estimate=pl.CostEstimate(flops=flops, bytes_accessed=2 * width * 5120, transcendentals=0),
     )(
-        tokens[0], wa, wb, cos_table, sin_table, starts, qk_scale[None], attn_rate[None], mlp_rate[None],
-        up_scale.reshape(PARTS, 1, hid), gate_scale.reshape(PARTS, 1, hid),
-    )
-    return out[None]
+        tokens, wa, wb, table, vectors
+    )
+    return out
 
 
 def body(*arrays):
     depth, tile = arrays[1].shape[0], arrays[0].shape[1] // lax.axis_size("tp")
-    aligned = depth % 16 == 0 and tile % 64 == 0 and arrays[3].shape[2] % (128 * PARTS) == 0
+    aligned = lax.axis_size("tp") == 4 and depth % 16 == 0 and tile % 64 == 0 and arrays[3].shape[2] % (128 * PARTS) == 0
     return fused_body(*arrays) if aligned else plain_body(*arrays)
 
 

time: 272 us -> 253 us (0.930)
  Pallas kernels: 251 us -> 235 us
    pallas_call x1, Pallas kernels: 251 us -> 235 us  [fused_body(): pl.pallas_call(lambda *refs: fused_kernel(reps, tps, cps, *refs), out_sha...]
    broadcast_in_dim x4 -> x3, local copies, waits for them, and re-layouts: 3.85 us -> 0.85 us  [the longest x1 0.62 us: fused_body(): jnp.concatenate([attn_rate, mlp_rate, up_scale, gate_scale, qk_scale])[None]]
where the time goes in v2:
time: 253 us; the launch traced here: 252 us
  Pallas kernels  235 us (93%)
  local copies, waits for them, and re-layouts  11.2 us (4%)
  other arithmetic  6.1 us (2%)
    pallas_call x1, Pallas kernels, fused_body(): pl.pallas_call(lambda *refs: fused_kernel(reps, tps, cps, *refs), out_sha...  235 us

profile of v2, /device:TPU:17, one launch (start us, length us, event | category | flops | bytes accessed | tf_op | source)
XLA Modules:
  0.0 252.1 jit_solution(11201971252805202070)
XLA Ops:
  0.0 1.2 slice.19
  1.2 1.5 add_select_fusion
  2.7 0.3 reduce-window.9
  3.1 0.1 slice_reduce_fusion
  3.3 0.1 subtract_convert_fusion
  3.4 1.5 multiply_sine_fusion
  5.0 0.2 broadcast_in_dim.18
  5.2 1.4 concatenate.22.refs_3_
  6.5 0.2 copy-done
  6.7 0.6 convert_element_type.24
  7.4 0.9 reshape.84
  8.3 0.9 copy.18
  9.3 0.5 reshape.85
  9.8 0.6 copy-done.1
  10.5 1.1 pad_maximum_fusion.refs_2_
  11.6 0.2 copy-done.2
  11.9 0.3 copy.16
  12.2 0.3 convert_element_type.22
  12.5 0.3 copy-done.4
  12.9 0.9 pad_maximum_fusion.1.refs_1_
  13.7 1.1 copy.20.refs_0_
  14.9 0.6 broadcast_in_dim.19.refs_4_
  15.5 234.5 %shard_map.109 = bf16[1,768,320]{2,1,0:T(8,128)(2,1)} custom-call(bf16[1,768,320]{2,1,0:T(8,128)(2,1)} %copy.20.refs_0_, bf16[160,1280]{1,0:T(8,128)(2,1)} %pad_maximum_fusion.1.refs_1_, bf16[5,160,768]{2,1,0:T(8,128)(2,1)} %pad_maximum_fusion.refs_2_, f32[4,192,256]{2,1,0:T(8,128)} %concatenate.22.refs_3_, f32[1,5440]{1,0:T(1,128)} %broadcast_in_dim.19.refs_4_), custom_call_target="tpu_custom_call" | custom-call | flops 10758389760 | bytes 13107200 | tf_op jit(solution)/shard_map/pallas_call | solution.py:562
  250.0 2.1 copy.21
  (33 shorter events, 0.6 us)
Async XLA Ops:
  5.1 1.6 copy-start
  9.2 1.1 copy-start.1
  10.5 1.4 copy-start.2
  11.9 0.9 copy-start.4
  11.9 1.8 copy-start.3
  12.8 2.0 copy-start.5
  12.8 2.0 copy-start.6
  12.8 2.0 copy-start.7
  12.8 2.0 copy-start.8
  12.8 2.0 copy-start.9

commit v3 on v2

--- a/solution.py
+++ b/solution.py
@@ -174,9 +174,9 @@
 
 def fused_kernel(
     reps, tps, cps,
-    tok_all, wa_ref, wb_ref, table_ref, vec_ref,
+    tok_all, qkv_ref, outs_ref, gu_ref, down_ref, vec_ref,
     out_all,
-    tok, xt, wa, wb, wo, csa, q_s, kv, near, far, xm, mix, macc, kept_part, near2, far2, obuf, fin,
+    table_ref, tok, xt, wa, wb, wo, csa, q_s, kv, near, far, xm, mix, macc, kept_part, near2, far2, obuf, fin,
     tok_send, tok_recv, w_send_z, w_send_y, w_recv, kv_send, kv_recv,
     a_send, a_recv, m_send, m_recv, b_send, b_recv, o_send, o_recv,
 ):
@@ -221,41 +221,55 @@
     def slot(j, s):
         return wa.at[s] if j is None else wb.at[j, s]
 
-    def own(j):
-        return wa_ref if j is None else wb_ref.at[j]
+    def near_cp(k):
+        if k == 1:
+            return c + 1 - 2 * lax.rem(c, 2)
+        return jnp.where(c < 2, k, 3 - k)
+
+    inner_cp = (c == 1) | (c == 2)
 
     def row(j):
         return 0 if j is None else j + 1
 
-    def z_copy(j, d):
-        return remote(own(j), slot(j, mine), w_send_z.at[row(j), d], w_recv.at[row(j), mine], (r, t, cp_peer(d)))
+    def z_copy(j, k):
+        part = slot(j, mine)
+        return remote(part, part, w_send_z.at[row(j), k], w_recv.at[row(j), mine], (r, t, near_cp(k)))
+
+    def z_relay(j):
+        s = r * cps + near_cp(3)
+        part = slot(j, s)
+        return remote(part, part, w_send_z.at[row(j), 0], w_recv.at[row(j), s], (r, t, near_cp(1)))
 
     def y_copy(j, k, d):
-        s = r * cps + cp_peer(k)
-        source = own(j) if k == 0 else slot(j, s)
-        return remote(source, slot(j, s), w_send_y.at[row(j), k, d], w_recv.at[row(j), s], (rep_peer(d), t, c))
+        s = mine if k == 0 else r * cps + near_cp(k)
+        part = slot(j, s)
+        return remote(part, part, w_send_y.at[row(j), k, d], w_recv.at[row(j), s], (rep_peer(d), t, c))
 
     def arrive(j, s):
-        remote(own(j), slot(j, s), w_send_z.at[row(j), 0], w_recv.at[row(j), s], (r, t, cp_peer(1))).wait_recv()
+        part = slot(j, s)
+        remote(part, part, w_send_z.at[row(j), 0], w_recv.at[row(j), s], (r, t, near_cp(1))).wait_recv()
 
     def send_own(j):
         for d in range(1, reps):
             y_copy(j, 0, d).start()
-        for d in range(1, cps):
-            z_copy(j, d).start()
-
-    def comm_step(j, k):
-        arrive(j, r * cps + cp_peer(k))
-        for d in range(1, reps):
-            y_copy(j, k, d).start()
+        z_copy(j, 1).start()
+        z_copy(j, 2).start()
+
+        @pl.when(inner_cp)
+        def _():
+            z_copy(j, 3).start()
 
     def comm_part(j):
-        @pl.when(j + 2 < PARTS)
-        def _():
-            send_own(j + 2)
-
         for k in range(1, cps):
-            comm_step(j, k)
+            arrive(j, r * cps + near_cp(k))
+            if k == 3:
+
+                @pl.when(inner_cp)
+                def _():
+                    z_relay(j).start()
+
+            for d in range(1, reps):
+                y_copy(j, k, d).start()
 
     def finish_part(j):
         for d in range(1, reps):
@@ -263,8 +277,14 @@
                 arrive(j, rep_peer(d) * cps + cp_peer(k))
 
     def drain(j):
-        for d in range(1, cps):
-            z_copy(j, d).wait_send()
+        z_copy(j, 1).wait_send()
+        z_copy(j, 2).wait_send()
+
+        @pl.when(inner_cp)
+        def _():
+            z_copy(j, 3).wait_send()
+            z_relay(j).wait_send()
+
         for d in range(1, reps):
             for k in range(cps):
                 y_copy(j, k, d).wait_send()
@@ -272,28 +292,46 @@
     def tok_copy(d):
         return remote(tok_ref, tok.at[t], tok_send.at[d], tok_recv.at[t], (r, tp_peer(d), c))
 
+    wa[mine, :, : 3 * local] = qkv_ref[...]
+    wa[mine, :, 3 * local :] = outs_ref[...]
+    send_own(None)
     for d in range(1, tps):
         tok_copy(d).start()
-    send_own(None)
     tok[t] = tok_ref[...]
-    wa[mine] = wa_ref[...]
-
-    @pl.loop(0, PARTS)
-    def _(j):
-        wb[j, mine] = wb_ref[j]
-
+    for j in range(PARTS):
+        wb[j, mine, :, :hid] = gu_ref[:, j * hid : (j + 1) * hid]
+        wb[j, mine, :, hid : 2 * hid] = gu_ref[:, hidden + j * hid : hidden + (j + 1) * hid]
+        wb[j, mine, :, 2 * hid :] = down_ref[:, j * hid : (j + 1) * hid]
+
+    segments_at = 2 * width + 2 * hidden
+    rates_at = segments_at + kv.shape[0]
+    qks_at = rates_at + 2 * HD
+    window = BACK + tile
+    for i in range(tps):
+        begin = segments_at + i * tile
+        key_ids = vec_ref[:, begin : begin + window]
+        square = (tile, tile)
+        diagonal_only = lax.broadcasted_iota(jnp.int32, square, 0) == lax.broadcasted_iota(jnp.int32, square, 1)
+        own_ids = jnp.sum(jnp.where(diagonal_only, key_ids[:, BACK:], 0.0), axis=1, keepdims=True)
+        column = lax.broadcasted_iota(jnp.int32, (tile, window), 1)
+        line = lax.broadcasted_iota(jnp.int32, (tile, window), 0) + BACK
+        earlier = (key_ids == own_ids) & (column < line)
+        position = jnp.sum(jnp.where(earlier, 1.0, 0.0), axis=1, keepdims=True)
+        angles = position * vec_ref[:, rates_at : rates_at + HD]
+        left = lax.broadcasted_iota(jnp.int32, (tile, HD), 1) < HD // 2
+        sine = jnp.sin(angles)
+        begins = lax.broadcasted_iota(jnp.int32, (tile, 2 * HD), 0).astype(jnp.float32) + BACK - position
+        table_ref[i] = jnp.concatenate([jnp.cos(angles), jnp.where(left, -sine, sine), begins], axis=1)
+
+    comm_part(None)
+    send_own(0)
     for d in range(1, tps):
         s = tp_peer(d)
         remote(tok_ref, tok.at[s], tok_send.at[d], tok_recv.at[s], (r, s, c)).wait_recv()
-    for k in range(1, cps):
-        comm_step(None, k)
-    send_own(0)
     finish_part(None)
-    send_own(1)
     csa[...] = column_scale(wa, shards)
     wo[...] = wa[:, :, 3 * local :].reshape(width, local)
 
-    qks_at = 2 * width + 2 * hidden
     rows_all = kv.shape[0]
 
     def kv_copy():
@@ -331,6 +369,10 @@
         def _():
             kv_copy().start()
 
+        @pl.when(step == (BACK - 1) // tile)
+        def _():
+            comm_part(0)
+
         return carry
 
     @pl.when(c == 0)
@@ -343,7 +385,7 @@
     def _():
         kv_copy().wait_recv()
 
-    window = BACK + tile
+    send_own(1)
 
     def near_copy(buf, k, send, recv):
         return remote(buf.at[k], buf.at[2 + k], send.at[k], recv.at[k], (r, beside, c))
@@ -391,7 +433,7 @@
         first = pl.ds(pl.multiple_of(i * tile, 64), window)
         column = lax.broadcasted_iota(jnp.int32, (tile, window), 1)
         line = lax.broadcasted_iota(jnp.int32, (tile, window), 0) + BACK
-        allowed = (column <= line) & (column >= table_ref[i, :, 2 * HD : 2 * HD + 1].astype(jnp.int32) - i * tile)
+        allowed = (column <= line) & (column >= table_ref[i, :, 2 * HD : 2 * HD + 1].astype(jnp.int32))
         qt = q_s[i]
         outs = []
         for h in range(heads):
@@ -409,9 +451,13 @@
         part = lax.dot_general(att, wo[...], NT, preferred_element_type=jnp.float32)
         scatter_step(step, part, mix, near, far, a_send, a_recv)
 
-        @pl.when(lax.rem(step, 2) == 0)
-        def _():
-            comm_part(step // 2)
+        @pl.when(lax.rem(step, 2) == 1)
+        def _():
+            comm_part(1 + step // 2)
+
+        @pl.when(step < PARTS - 2)
+        def _():
+            send_own(step + 2)
 
         return carry
 
@@ -432,7 +478,6 @@
     mix_copy(0, t, across).start()
     mix_copy(1, t, beside).start()
     macc[...] = jnp.zeros_like(macc)
-    comm_part(2)
     mix_copy(0, across, across).wait_recv()
     mix_copy(2, across, beside).start()
     mix_copy(1, beside, beside).wait_recv()
@@ -538,23 +583,16 @@
     width = depth * shards
     tile = rows // tps
     bf16 = jnp.bfloat16
-    wa = jnp.concatenate(
-        [qkv_weight.reshape(depth, 3 * local).astype(bf16), out_weight.astype(bf16).T], axis=1
-    )
-    gu = gate_up_weight.astype(bf16).reshape(depth, 2, PARTS, hid).transpose(2, 0, 1, 3)
-    down = down_weight.astype(bf16).reshape(PARTS, hid, depth).transpose(0, 2, 1)
-    wb = jnp.concatenate([gu.reshape(PARTS, depth, 2 * hid), down], axis=2)
-    position = stream_positions(segment_ids[0])
-    own_pos = lax.dynamic_slice_in_dim(position, lax.axis_index("cp") * rows, rows)
+    cp = lax.axis_index("cp")
+    qkv = qkv_weight.reshape(depth, 3 * local).astype(bf16)
+    gate_up = gate_up_weight.reshape(depth, 2 * hidden).astype(bf16)
+    padded = jnp.concatenate([jnp.full((BACK,), -1.0, jnp.float32), segment_ids[0].astype(jnp.float32)])
+    window = lax.dynamic_slice_in_dim(padded, cp * rows, BACK + rows)
     half = HD // 2
     frequency = jnp.exp(-math.log(10000.0) * jnp.arange(half, dtype=jnp.float32) * 2.0 / HD)
-    angles = own_pos.astype(jnp.float32)[:, None] * frequency[None, :]
-    cosine, sine = jnp.cos(angles), jnp.sin(angles)
-    first = (BACK + jnp.arange(rows, dtype=jnp.int32) - own_pos).astype(jnp.float32)[:, None]
-    table = jnp.concatenate(
-        [cosine, cosine, -sine, sine, jnp.broadcast_to(first, (rows, 2 * HD))], axis=1
-    ).reshape(tps, tile, 4 * HD)
-    vectors = jnp.concatenate([attn_rate, mlp_rate, up_scale, gate_scale, qk_scale])[None]
+    vectors = jnp.concatenate(
+        [attn_rate, mlp_rate, up_scale, gate_scale, window, frequency, frequency, frequency, frequency, qk_scale]
+    )[None]
     vmem = pl.BlockSpec(memory_space=pltpu.VMEM)
     dma = pltpu.SemaphoreType.DMA
     f32 = jnp.float32
@@ -562,9 +600,10 @@
     out = pl.pallas_call(
         lambda *refs: fused_kernel(reps, tps, cps, *refs),
         out_shape=jax.ShapeDtypeStruct((1, rows, local), bf16),
-        in_specs=[vmem] * 5,
+        in_specs=[vmem] * 6,
         out_specs=vmem,
         scratch_shapes=[
+            pltpu.VMEM((tps, tile, 4 * HD), f32),
             pltpu.VMEM((tps, rows, local), bf16),
             pltpu.VMEM((tps, tile, width), bf16),
             pltpu.VMEM((shards, depth, 4 * local), bf16),
@@ -594,14 +633,14 @@
         ),
         cost_estimate=pl.CostEstimate(flops=flops, bytes_accessed=2 * width * 5120, transcendentals=0),
     )(
-        tokens, wa, wb, table, vectors
+        tokens, qkv, out_weight.astype(bf16).T, gate_up, down_weight.astype(bf16).T, vectors
     )
     return out
 
 
 def body(*arrays):
     depth, tile = arrays[1].shape[0], arrays[0].shape[1] // lax.axis_size("tp")
-    aligned = lax.axis_size("tp") == 4 and depth % 16 == 0 and tile % 64 == 0 and arrays[3].shape[2] % (128 * PARTS) == 0
+    aligned = lax.axis_size("tp") == 4 and lax.axis_size("cp") == 4 and depth % 16 == 0 and tile % 64 == 0 and arrays[3].shape[2] % (128 * PARTS) == 0
     return fused_body(*arrays) if aligned else plain_body(*arrays)
 
 

time: 253 us -> 216 us (0.85)
  the two profiles are of different devices: /device:TPU:17 before, /device:TPU:1 now
where the time goes in v3:
time: 216 us
  Pallas kernels  205 us (95%)
  local copies, waits for them, and re-layouts  7.03 us (3%)
  other arithmetic  4.29 us (2%)
    pallas_call x1, Pallas kernels, fused_body(): pl.pallas_call(lambda *refs: fused_kernel(reps, tps, cps, *refs), out_sha...  205 us

profile of v3, /device:TPU:1, one launch (start us, length us, event | category | flops | bytes accessed | tf_op | source)
XLA Modules:
  0.0 215.9 jit_solution(15306585894588814147)
XLA Ops:
  0.0 0.7 convert_element_type.28
  0.7 0.1 pad_dynamic-slice_fusion
  0.8 0.8 concatenate.7
  1.6 0.6 broadcast_in_dim.4.refs_5_
  2.3 0.0 copy-start.1
  2.3 2.1 convert_element_type.25
  4.3 1.0 copy.18
  5.3 0.0 copy-start.2
  5.3 0.0 copy-done.1
  5.4 0.0 copy-start
  5.4 0.3 copy.15
  5.7 0.0 copy-start.3
  5.7 1.1 convert_element_type.23.refs_1_
  6.8 0.0 copy-done.2
  6.8 1.1 copy.16.refs_0_
  7.8 0.0 copy-done
  7.8 0.8 convert_bitcast_fusion.refs_4_
  8.6 0.0 copy-done.3
  8.6 0.7 convert_bitcast_fusion.1.refs_2_
  9.3 204.5 %shard_map.109 = bf16[1,768,320]{2,1,0:T(8,128)(2,1)} custom-call(bf16[1,768,320]{2,1,0:T(8,128)(2,1)} %copy.16.refs_0_, bf16[160,960]{1,0:T(8,128)(2,1)} %convert_element_type.23.refs_1_, bf16[160,320]{1,0:T(8,128)(2,1)} %convert_bitcast_fusion.1.refs_2_, bf16[160,2560]{1,0:T(8,128)(2,1)} %bitcast.8, bf16[160,1280]{1,0:T(8,128)(2,1)} %convert_bitcast_fusion.refs_4_, ...), custom_call_target="tpu_custom_call" | custom-call | flops 10758389760 | bytes 13107200 | tf_op jit(solution)/shard_map/pallas_call | solution.py:600
  213.8 2.1 copy.17
  (2 shorter events, 0.1 us)
Async XLA Ops:
  2.3 3.1 %copy-start.1 = (f32[160,3,320]{2,0,1:T(8,128)S(1)}, f32[160,3,320]{2,0,1:T(8,128)}, u32[]{:S(2)}) copy-start(f32[160,3,320]{2,0,1:T(8,128)} %param.12) | copy-start | bytes 1843204
  5.3 1.4 copy-start.2
  5.4 2.5 %copy-start = (f32[1280,160]{0,1:T(8,128)S(1)}, f32[1280,160]{0,1:T(8,128)}, u32[]{:S(2)}) copy-start(f32[1280,160]{0,1:T(8,128)} %param.15) | copy-start | bytes 2457604
  5.7 3.0 %copy-start.3 = (f32[320,160]{0,1:T(8,128)S(1)}, f32[320,160]{0,1:T(8,128)}, u32[]{:S(2)}) copy-start(f32[320,160]{0,1:T(8,128)} %param.13) | copy-start | bytes 614404

commit v4 on v3

--- a/solution.py
+++ b/solution.py
@@ -1,3 +1,4 @@
+import functools
 import math
 
 import jax
@@ -159,6 +160,7 @@
 
 MESH = pl.DeviceIdType.MESH
 PARTS = 5
+SWAPPED = (2, 4)
 BACK = 512
 NT = (((1,), (1,)), ((), ()))
 
@@ -249,9 +251,16 @@
         part = slot(j, s)
         remote(part, part, w_send_z.at[row(j), 0], w_recv.at[row(j), s], (r, t, near_cp(1))).wait_recv()
 
-    def send_own(j):
+    def swap_copy(j):
+        s = rep_peer(1) * cps + c
+        part = slot(j, s)
+        return remote(part, part, w_send_y.at[row(j), 1, 0], w_recv.at[row(j), s], (r, t, near_cp(1)))
+
+    def send_y(j):
         for d in range(1, reps):
             y_copy(j, 0, d).start()
+
+    def send_z(j):
         z_copy(j, 1).start()
         z_copy(j, 2).start()
 
@@ -260,6 +269,9 @@
             z_copy(j, 3).start()
 
     def comm_part(j):
+        if j in SWAPPED:
+            arrive(j, rep_peer(1) * cps + c)
+            swap_copy(j).start()
         for k in range(1, cps):
             arrive(j, r * cps + near_cp(k))
             if k == 3:
@@ -268,13 +280,22 @@
                 def _():
                     z_relay(j).start()
 
-            for d in range(1, reps):
-                y_copy(j, k, d).start()
+            if k > 1 or j not in SWAPPED:
+                for d in range(1, reps):
+                    y_copy(j, k, d).start()
 
     def finish_part(j):
         for d in range(1, reps):
-            for k in range(cps):
+            for k in range(1, cps):
                 arrive(j, rep_peer(d) * cps + cp_peer(k))
+
+            if j is None:
+                arrive(j, rep_peer(d) * cps + c)
+            else:
+
+                @pl.when(functools.reduce(lambda a, b: a & b, [j != q for q in SWAPPED]))
+                def _():
+                    arrive(j, rep_peer(d) * cps + c)
 
     def drain(j):
         z_copy(j, 1).wait_send()
@@ -287,14 +308,18 @@
 
         for d in range(1, reps):
             for k in range(cps):
-                y_copy(j, k, d).wait_send()
+                if k == 1 and j in SWAPPED:
+                    swap_copy(j).wait_send()
+                else:
+                    y_copy(j, k, d).wait_send()
 
     def tok_copy(d):
         return remote(tok_ref, tok.at[t], tok_send.at[d], tok_recv.at[t], (r, tp_peer(d), c))
 
     wa[mine, :, : 3 * local] = qkv_ref[...]
     wa[mine, :, 3 * local :] = outs_ref[...]
-    send_own(None)
+    send_y(None)
+    send_z(None)
     for d in range(1, tps):
         tok_copy(d).start()
     tok[t] = tok_ref[...]
@@ -324,19 +349,30 @@
         table_ref[i] = jnp.concatenate([jnp.cos(angles), jnp.where(left, -sine, sine), begins], axis=1)
 
     comm_part(None)
-    send_own(0)
+    send_z(0)
+    for j in range(3):
+        send_y(j)
     for d in range(1, tps):
         s = tp_peer(d)
         remote(tok_ref, tok.at[s], tok_send.at[d], tok_recv.at[s], (r, s, c)).wait_recv()
     finish_part(None)
     csa[...] = column_scale(wa, shards)
     wo[...] = wa[:, :, 3 * local :].reshape(width, local)
+    comm_part(0)
 
     rows_all = kv.shape[0]
 
-    def kv_copy():
+    kv_pieces = -(-BACK // tile)
+
+    def kv_copy(piece):
+        count = min(tile, BACK - piece * tile)
+        taken = piece * tile + count
         return remote(
-            kv.at[pl.ds(rows_all - BACK, BACK)], kv.at[pl.ds(0, BACK)], kv_send, kv_recv, (r, t, cp_peer(1))
+            kv.at[pl.ds(rows_all - taken, count)],
+            kv.at[pl.ds(BACK - taken, count)],
+            kv_send.at[piece],
+            kv_recv.at[piece],
+            (r, t, cp_peer(1)),
         )
 
     def project(step, carry):
@@ -365,13 +401,17 @@
             [rope(local, 1.0), pr[:, 2 * local :]], axis=1
         ).astype(jnp.bfloat16)
 
-        @pl.when((step == (BACK - 1) // tile) & (c < cps - 1))
-        def _():
-            kv_copy().start()
-
-        @pl.when(step == (BACK - 1) // tile)
-        def _():
-            comm_part(0)
+        for piece in range(kv_pieces):
+
+            @pl.when((step == piece) & (c < cps - 1))
+            def _():
+                kv_copy(piece).start()
+
+        @pl.when(step == kv_pieces - 1)
+        def _():
+            send_z(1)
+            send_y(3)
+            send_y(4)
 
         return carry
 
@@ -383,9 +423,10 @@
 
     @pl.when(c > 0)
     def _():
-        kv_copy().wait_recv()
-
-    send_own(1)
+        for piece in range(kv_pieces):
+            kv_copy(piece).wait_recv()
+
+    send_z(2)
 
     def near_copy(buf, k, send, recv):
         return remote(buf.at[k], buf.at[2 + k], send.at[k], recv.at[k], (r, beside, c))
@@ -451,17 +492,19 @@
         part = lax.dot_general(att, wo[...], NT, preferred_element_type=jnp.float32)
         scatter_step(step, part, mix, near, far, a_send, a_recv)
 
-        @pl.when(lax.rem(step, 2) == 1)
-        def _():
-            comm_part(1 + step // 2)
-
-        @pl.when(step < PARTS - 2)
-        def _():
-            send_own(step + 2)
+        @pl.when(step == 1)
+        def _():
+            send_z(3)
+
+        @pl.when(step == 2)
+        def _():
+            comm_part(1)
+            send_z(4)
 
         return carry
 
     lax.fori_loop(0, tps, attend, 0)
+    comm_part(2)
 
     def unit(v):
         return v * lax.rsqrt(jnp.sum(v * v, axis=1, keepdims=True) + EPS)
@@ -480,9 +523,9 @@
     macc[...] = jnp.zeros_like(macc)
     mix_copy(0, across, across).wait_recv()
     mix_copy(2, across, beside).start()
+    comm_part(3)
     mix_copy(1, beside, beside).wait_recv()
     mix_copy(2, diagonal, beside).wait_recv()
-    comm_part(3)
 
     def scales(j):
         cs = column_scale(wb.at[j], shards)
@@ -550,8 +593,7 @@
 
     drain(None)
 
-    @pl.loop(0, PARTS)
-    def _(j):
+    for j in range(PARTS):
         drain(j)
 
     for d in range(1, tps):
@@ -567,7 +609,8 @@
 
     @pl.when(c < cps - 1)
     def _():
-        kv_copy().wait_send()
+        for piece in range(kv_pieces):
+            kv_copy(piece).wait_send()
 
 
 def fused_body(
@@ -624,7 +667,7 @@
             pltpu.VMEM((tps, tile, local), bf16),
             dma((tps,)), dma((tps,)),
             dma((PARTS + 1, cps)), dma((PARTS + 1, cps, reps)), dma((PARTS + 1, shards)),
-            dma, dma,
+            dma((-(-BACK // tile),)), dma((-(-BACK // tile),)),
             dma((tps,)), dma((tps,)), dma((tps,)), dma((tps,)),
             dma((tps,)), dma((tps,)), dma((tps,)), dma((tps,)),
         ],
@@ -640,7 +683,7 @@
 
 def body(*arrays):
     depth, tile = arrays[1].shape[0], arrays[0].shape[1] // lax.axis_size("tp")
-    aligned = lax.axis_size("tp") == 4 and lax.axis_size("cp") == 4 and depth % 16 == 0 and tile % 64 == 0 and arrays[3].shape[2] % (128 * PARTS) == 0
+    aligned = lax.axis_size("tp") == 4 and lax.axis_size("cp") == 4 and lax.axis_size("rep") == 2 and depth % 16 == 0 and tile % 64 == 0 and arrays[3].shape[2] % (128 * PARTS) == 0
     return fused_body(*arrays) if aligned else plain_body(*arrays)
 
 

time: 216 us -> 207 us (0.958)
  Pallas kernels: 205 us -> 195 us
    pallas_call x1, Pallas kernels: 205 us -> 195 us  [fused_body(): pl.pallas_call(lambda *refs: fused_kernel(reps, tps, cps, *refs), out_sha...]
where the time goes in v4:
time: 207 us; the launch traced here: 206 us
  Pallas kernels  195 us (94%)
  local copies, waits for them, and re-layouts  7.03 us (3%)
  other arithmetic  4.29 us (2%)
    pallas_call x1, Pallas kernels, fused_body(): pl.pallas_call(lambda *refs: fused_kernel(reps, tps, cps, *refs), out_sha...  195 us

profile of v4, /device:TPU:1, one launch (start us, length us, event | category | flops | bytes accessed | tf_op | source)
XLA Modules:
  0.0 206.2 jit_solution(15378633585317711133)
XLA Ops:
  0.0 0.7 convert_element_type.28
  0.7 0.1 pad_dynamic-slice_fusion
  0.8 0.8 concatenate.7
  1.6 0.6 broadcast_in_dim.4.refs_5_
  2.3 0.0 copy-start.1
  2.3 2.1 %convert_element_type.25 = bf16[160,2,1280]{2,1,0:T(2,128)(2,1)S(1)} convert(f32[160,2,1280]{2,1,0:T(2,128)} %param.14) | non-fusion elementwise | flops 409600 | bytes 2457600 | tf_op jit(solution)/shard_map/convert_element_type | solution.py:631
  4.3 1.0 copy.18
  5.3 0.0 copy-start.2
  5.3 0.0 copy-done.1
  5.4 0.0 copy-start
  5.4 0.3 copy.15
  5.7 0.0 copy-start.3
  5.7 1.1 convert_element_type.23.refs_1_
  6.8 0.0 copy-done.2
  6.8 1.1 copy.16.refs_0_
  7.8 0.0 copy-done
  7.8 0.8 convert_bitcast_fusion.refs_4_
  8.6 0.0 copy-done.3
  8.6 0.7 convert_bitcast_fusion.1.refs_2_
  9.3 194.9 %shard_map.109 = bf16[1,768,320]{2,1,0:T(8,128)(2,1)} custom-call(bf16[1,768,320]{2,1,0:T(8,128)(2,1)} %copy.16.refs_0_, bf16[160,960]{1,0:T(8,128)(2,1)} %convert_element_type.23.refs_1_, bf16[160,320]{1,0:T(8,128)(2,1)} %convert_bitcast_fusion.1.refs_2_, bf16[160,2560]{1,0:T(8,128)(2,1)} %bitcast.8, bf16[160,1280]{1,0:T(8,128)(2,1)} %convert_bitcast_fusion.refs_4_, ...), custom_call_target="tpu_custom_call" | custom-call | flops 10758389760 | bytes 13107200 | tf_op jit(solution)/shard_map/pallas_call | solution.py:643
  204.2 2.1 %copy.17 = bf16[1,768,320]{1,2,0:T(8,128)(2,1)} copy(bf16[1,768,320]{2,1,0:T(8,128)(2,1)} %shard_map.109) | data formatting | bytes 983040 | tf_op jit(solution)/shard_map/pallas_call | solution.py:643
  (2 shorter events, 0.1 us)
Async XLA Ops:
  2.3 3.1 %copy-start.1 = (f32[160,3,320]{2,0,1:T(8,128)S(1)}, f32[160,3,320]{2,0,1:T(8,128)}, u32[]{:S(2)}) copy-start(f32[160,3,320]{2,0,1:T(8,128)} %param.12) | copy-start | bytes 1843204
  5.3 1.4 copy-start.2
  5.4 2.5 %copy-start = (f32[1280,160]{0,1:T(8,128)S(1)}, f32[1280,160]{0,1:T(8,128)}, u32[]{:S(2)}) copy-start(f32[1280,160]{0,1:T(8,128)} %param.15) | copy-start | bytes 2457604
  5.7 3.0 %copy-start.3 = (f32[320,160]{0,1:T(8,128)S(1)}, f32[320,160]{0,1:T(8,128)}, u32[]{:S(2)}) copy-start(f32[320,160]{0,1:T(8,128)} %param.13) | copy-start | bytes 614404

commit v5 on v4

--- a/solution.py
+++ b/solution.py
@@ -176,9 +176,9 @@
 
 def fused_kernel(
     reps, tps, cps,
-    tok_all, qkv_ref, outs_ref, gu_ref, down_ref, vec_ref,
-    out_all,
-    table_ref, tok, xt, wa, wb, wo, csa, q_s, kv, near, far, xm, mix, macc, kept_part, near2, far2, obuf, fin,
+    tok_all, qkv_all, outs_all, gu_all, down_all, vec_ref,
+    out_ref,
+    tok_raw, qkv_raw, outs_raw, gu_raw, down_raw, load, table_ref, tok, xt, wa, wb, wo, csa, q_s, kv, near, far, xm, mix, macc, kept_part, near2, far2, obuf, fin,
     tok_send, tok_recv, w_send_z, w_send_y, w_recv, kv_send, kv_recv,
     a_send, a_recv, m_send, m_recv, b_send, b_recv, o_send, o_recv,
 ):
@@ -192,7 +192,7 @@
     hid = wb.shape[3] // 3
     mine = r * cps + c
     hidden = PARTS * hid
-    tok_ref, out_ref = tok_all.at[0], out_all.at[0]
+    tok_ref = tok.at[t]
     beside = t + 1 - 2 * lax.rem(t, 2)
     across = lax.rem(t + 2, tps)
     diagonal = lax.rem(beside + 2, tps)
@@ -206,6 +206,14 @@
     def rep_peer(d):
         return lax.rem(r + d, reps)
 
+    loads = [
+        pltpu.make_async_copy(source, place, load.at[i])
+        for i, (source, place) in enumerate(
+            [(qkv_all, qkv_raw), (outs_all, outs_raw), (tok_all, tok_raw), (gu_all, gu_raw), (down_all, down_raw)]
+        )
+    ]
+    for copy in loads:
+        copy.start()
     barrier = pltpu.get_barrier_semaphore()
     for d in range(1, tps):
         pl.semaphore_signal(barrier, inc=1, device_id=(r, tp_peer(d), c), device_id_type=MESH)
@@ -263,10 +271,13 @@
     def send_z(j):
         z_copy(j, 1).start()
         z_copy(j, 2).start()
-
-        @pl.when(inner_cp)
-        def _():
+        if j in SWAPPED:
             z_copy(j, 3).start()
+        else:
+
+            @pl.when(inner_cp)
+            def _():
+                z_copy(j, 3).start()
 
     def comm_part(j):
         if j in SWAPPED:
@@ -274,7 +285,7 @@
             swap_copy(j).start()
         for k in range(1, cps):
             arrive(j, r * cps + near_cp(k))
-            if k == 3:
+            if k == 3 and j not in SWAPPED:
 
                 @pl.when(inner_cp)
                 def _():
@@ -301,10 +312,14 @@
         z_copy(j, 1).wait_send()
         z_copy(j, 2).wait_send()
 
-        @pl.when(inner_cp)
-        def _():
+        if j in SWAPPED:
             z_copy(j, 3).wait_send()
-            z_relay(j).wait_send()
+        else:
+
+            @pl.when(inner_cp)
+            def _():
+                z_copy(j, 3).wait_send()
+                z_relay(j).wait_send()
 
         for d in range(1, reps):
             for k in range(cps):
@@ -316,17 +331,23 @@
     def tok_copy(d):
         return remote(tok_ref, tok.at[t], tok_send.at[d], tok_recv.at[t], (r, tp_peer(d), c))
 
-    wa[mine, :, : 3 * local] = qkv_ref[...]
-    wa[mine, :, 3 * local :] = outs_ref[...]
+    loads[0].wait()
+    loads[1].wait()
+    for kind in range(3):
+        wa[mine, :, kind * local : (kind + 1) * local] = qkv_raw[kind].astype(jnp.bfloat16)
+    wa[mine, :, 3 * local :] = outs_raw[...].astype(jnp.bfloat16)
     send_y(None)
     send_z(None)
+    loads[2].wait()
+    tok[t] = tok_raw[...].astype(jnp.float32).T.astype(jnp.bfloat16)
     for d in range(1, tps):
         tok_copy(d).start()
-    tok[t] = tok_ref[...]
+    loads[3].wait()
+    loads[4].wait()
     for j in range(PARTS):
-        wb[j, mine, :, :hid] = gu_ref[:, j * hid : (j + 1) * hid]
-        wb[j, mine, :, hid : 2 * hid] = gu_ref[:, hidden + j * hid : hidden + (j + 1) * hid]
-        wb[j, mine, :, 2 * hid :] = down_ref[:, j * hid : (j + 1) * hid]
+        wb[j, mine, :, :hid] = gu_raw[:, 0, j * hid : (j + 1) * hid].astype(jnp.bfloat16)
+        wb[j, mine, :, hid : 2 * hid] = gu_raw[:, 1, j * hid : (j + 1) * hid].astype(jnp.bfloat16)
+        wb[j, mine, :, 2 * hid :] = down_raw[:, j * hid : (j + 1) * hid].astype(jnp.bfloat16)
 
     segments_at = 2 * width + 2 * hidden
     rates_at = segments_at + kv.shape[0]
@@ -410,6 +431,7 @@
         @pl.when(step == kv_pieces - 1)
         def _():
             send_z(1)
+            send_z(2)
             send_y(3)
             send_y(4)
 
@@ -426,7 +448,7 @@
         for piece in range(kv_pieces):
             kv_copy(piece).wait_recv()
 
-    send_z(2)
+    send_z(3)
 
     def near_copy(buf, k, send, recv):
         return remote(buf.at[k], buf.at[2 + k], send.at[k], recv.at[k], (r, beside, c))
@@ -494,12 +516,11 @@
 
         @pl.when(step == 1)
         def _():
-            send_z(3)
+            send_z(4)
 
         @pl.when(step == 2)
         def _():
             comm_part(1)
-            send_z(4)
 
         return carry
 
@@ -588,8 +609,8 @@
     for d in range(1, tps):
         s = tp_peer(d)
         remote(obuf.at[t], fin.at[s], o_send.at[t], o_recv.at[s], (r, s, c)).wait_recv()
-    for s in range(tps):
-        out_ref[pl.ds(s * tile, tile), :] = fin[s]
+    whole = jnp.concatenate([fin[s] for s in range(tps)], axis=0)
+    out_ref[...] = whole.astype(jnp.float32).T.astype(jnp.bfloat16)
 
     drain(None)
 
@@ -627,8 +648,6 @@
     tile = rows // tps
     bf16 = jnp.bfloat16
     cp = lax.axis_index("cp")
-    qkv = qkv_weight.reshape(depth, 3 * local).astype(bf16)
-    gate_up = gate_up_weight.reshape(depth, 2 * hidden).astype(bf16)
     padded = jnp.concatenate([jnp.full((BACK,), -1.0, jnp.float32), segment_ids[0].astype(jnp.float32)])
     window = lax.dynamic_slice_in_dim(padded, cp * rows, BACK + rows)
     half = HD // 2
@@ -637,15 +656,22 @@
         [attn_rate, mlp_rate, up_scale, gate_scale, window, frequency, frequency, frequency, frequency, qk_scale]
     )[None]
     vmem = pl.BlockSpec(memory_space=pltpu.VMEM)
+    hbm = pl.BlockSpec(memory_space=pl.ANY)
     dma = pltpu.SemaphoreType.DMA
     f32 = jnp.float32
     flops = 2 * rows * width * (4 * local + 3 * hidden) + 4 * rows * (BACK + tile) * local
     out = pl.pallas_call(
         lambda *refs: fused_kernel(reps, tps, cps, *refs),
-        out_shape=jax.ShapeDtypeStruct((1, rows, local), bf16),
-        in_specs=[vmem] * 6,
+        out_shape=jax.ShapeDtypeStruct((local, rows), bf16),
+        in_specs=[hbm] * 5 + [vmem],
         out_specs=vmem,
         scratch_shapes=[
+            pltpu.VMEM((local, rows), bf16),
+            pltpu.VMEM((3, depth, local), f32),
+            pltpu.VMEM((depth, local), f32),
+            pltpu.VMEM((depth, 2, hidden), f32),
+            pltpu.VMEM((depth, hidden), f32),
+            dma((5,)),
             pltpu.VMEM((tps, tile, 4 * HD), f32),
             pltpu.VMEM((tps, rows, local), bf16),
             pltpu.VMEM((tps, tile, width), bf16),
@@ -676,9 +702,9 @@
         ),
         cost_estimate=pl.CostEstimate(flops=flops, bytes_accessed=2 * width * 5120, transcendentals=0),
     )(
-        tokens, qkv, out_weight.astype(bf16).T, gate_up, down_weight.astype(bf16).T, vectors
+        tokens[0].T, qkv_weight.transpose(1, 0, 2), out_weight.T, gate_up_weight, down_weight.T, vectors
     )
-    return out
+    return out.T[None]
 
 
 def body(*arrays):

time: 207 us -> 194 us (0.937)
  the two profiles are of different devices: /device:TPU:1 before, /device:TPU:25 now
where the time goes in v5:
time: 194 us
  Pallas kernels  190 us (98%)
  local copies, waits for them, and re-layouts  3.38 us (2%)
    pallas_call x1, Pallas kernels, fused_body(): pl.pallas_call(lambda *refs: fused_kernel(reps, tps, cps, *refs), out_sha...  190 us

profile of v5, /device:TPU:25, one launch (start us, length us, event | category | flops | bytes accessed | tf_op | source)
XLA Modules:
  0.0 193.8 jit_solution(1411344071534270010)
XLA Ops:
  0.0 0.7 convert_element_type.6
  0.7 0.1 pad_dynamic-slice_fusion
  0.8 0.8 concatenate.7
  1.6 0.6 broadcast_in_dim.7.refs_5_
  2.3 189.7 %shard_map.109 = bf16[320,768]{1,0:T(8,128)(2,1)} custom-call(bf16[320,768]{1,0:T(8,128)(2,1)} %bitcast.14, f32[3,160,320]{2,1,0:T(8,128)} %bitcast.13, f32[160,320]{1,0:T(8,128)} %bitcast.15, f32[160,2,1280]{2,1,0:T(2,128)} %refs_3_.1, f32[160,1280]{1,0:T(8,128)} %bitcast.12, f32[1,6848]{1,0:T(1,128)} %broadcast_in_dim.7.refs_5_), custom_call_target="tpu_custom_call" | custom-call | flops 10758389760 | bytes 13107200 | tf_op jit(solution)/shard_map/pallas_call | solution.py:663
  192.0 1.8 copy.13
  (1 shorter events, 0.0 us)

commit v6 on v5

--- a/solution.py
+++ b/solution.py
@@ -160,7 +160,7 @@
 
 MESH = pl.DeviceIdType.MESH
 PARTS = 5
-SWAPPED = (2, 4)
+SWAPPED = (3, 4)
 BACK = 512
 NT = (((1,), (1,)), ((), ()))
 
@@ -378,8 +378,9 @@
         remote(tok_ref, tok.at[s], tok_send.at[d], tok_recv.at[s], (r, s, c)).wait_recv()
     finish_part(None)
     csa[...] = column_scale(wa, shards)
+    comm_part(0)
+    send_z(1)
     wo[...] = wa[:, :, 3 * local :].reshape(width, local)
-    comm_part(0)
 
     rows_all = kv.shape[0]
 
@@ -430,7 +431,6 @@
 
         @pl.when(step == kv_pieces - 1)
         def _():
-            send_z(1)
             send_z(2)
             send_y(3)
             send_y(4)

time: 194 us -> 204 us (1.052)
  the two profiles are of different devices: /device:TPU:25 before, /device:TPU:1 now
where the time goes in v6:
time: 204 us
  Pallas kernels  200 us (98%)
  local copies, waits for them, and re-layouts  3.38 us (2%)
    pallas_call x1, Pallas kernels, fused_body(): pl.pallas_call(lambda *refs: fused_kernel(reps, tps, cps, *refs), out_sha...  200 us

profile of v6, /device:TPU:1, one launch (start us, length us, event | category | flops | bytes accessed | tf_op | source)
XLA Modules:
  0.0 204.1 jit_solution(4628306830789178267)
XLA Ops:
  0.0 0.7 convert_element_type.6
  0.7 0.1 pad_dynamic-slice_fusion
  0.8 0.8 concatenate.7
  1.6 0.6 broadcast_in_dim.7.refs_5_
  2.3 200.0 %shard_map.109 = bf16[320,768]{1,0:T(8,128)(2,1)} custom-call(bf16[320,768]{1,0:T(8,128)(2,1)} %bitcast.14, f32[3,160,320]{2,1,0:T(8,128)} %bitcast.13, f32[160,320]{1,0:T(8,128)} %bitcast.15, f32[160,2,1280]{2,1,0:T(2,128)} %refs_3_.1, f32[160,1280]{1,0:T(8,128)} %bitcast.12, f32[1,6848]{1,0:T(1,128)} %broadcast_in_dim.7.refs_5_), custom_call_target="tpu_custom_call" | custom-call | flops 10758389760 | bytes 13107200 | tf_op jit(solution)/shard_map/pallas_call | solution.py:663
  202.3 1.8 copy.13
  (1 shorter events, 0.0 us)

commit v7 on v5

--- a/solution.py
+++ b/solution.py
@@ -431,7 +431,6 @@
         @pl.when(step == kv_pieces - 1)
         def _():
             send_z(1)
-            send_z(2)
             send_y(3)
             send_y(4)
 
@@ -448,7 +447,7 @@
         for piece in range(kv_pieces):
             kv_copy(piece).wait_recv()
 
-    send_z(3)
+    send_z(2)
 
     def near_copy(buf, k, send, recv):
         return remote(buf.at[k], buf.at[2 + k], send.at[k], recv.at[k], (r, beside, c))
@@ -513,6 +512,10 @@
         att = (jnp.concatenate(outs, axis=1) * csa[:, 3 * local :]).astype(jnp.bfloat16)
         part = lax.dot_general(att, wo[...], NT, preferred_element_type=jnp.float32)
         scatter_step(step, part, mix, near, far, a_send, a_recv)
+
+        @pl.when(step == 0)
+        def _():
+            send_z(3)
 
         @pl.when(step == 1)
         def _():

time: 194 us -> 194 us (level)
  no operation moved by 1% of the time
where the time goes in v7:
time: 194 us
  Pallas kernels  190 us (98%)
  local copies, waits for them, and re-layouts  3.38 us (2%)
    pallas_call x1, Pallas kernels, fused_body(): pl.pallas_call(lambda *refs: fused_kernel(reps, tps, cps, *refs), out_sha...  190 us

profile of v7, /device:TPU:25, one launch (start us, length us, event | category | flops | bytes accessed | tf_op | source)
XLA Modules:
  0.0 193.8 jit_solution(4657490823545861145)
XLA Ops:
  0.0 0.7 convert_element_type.6
  0.7 0.1 pad_dynamic-slice_fusion
  0.8 0.8 concatenate.7
  1.6 0.6 broadcast_in_dim.7.refs_5_
  2.3 189.7 %shard_map.109 = bf16[320,768]{1,0:T(8,128)(2,1)} custom-call(bf16[320,768]{1,0:T(8,128)(2,1)} %bitcast.14, f32[3,160,320]{2,1,0:T(8,128)} %bitcast.13, f32[160,320]{1,0:T(8,128)} %bitcast.15, f32[160,2,1280]{2,1,0:T(2,128)} %refs_3_.1, f32[160,1280]{1,0:T(8,128)} %bitcast.12, f32[1,6848]{1,0:T(1,128)} %broadcast_in_dim.7.refs_5_), custom_call_target="tpu_custom_call" | custom-call | flops 10758389760 | bytes 13107200 | tf_op jit(solution)/shard_map/pallas_call | solution.py:666
  192.0 1.8 copy.13
  (1 shorter events, 0.0 us)
